TPU v7x, 32 devices: a whole 2x2x4 slice. The times are simulated.
32 devices in a mesh: row: 8 (over y, x, core), col: 4 (over z).
Axes of the slice: x: 2, y: 2, z: 4, core: 2. Of those that a mesh axis runs over, the one named last changes fastest.
Arguments:
- amplitudes: bfloat16 [8192, 8192], P('row', 'col'), may hold values from -6 to 6
- integrals: bfloat16 [8192, 1024], P('col', 'row'), may hold values from -0.0625 to 0.0625
- tile_mask: int32 [64, 64], P('row', 'col'), may hold values 0 or 1
Outputs:
- residual: bfloat16 [8192, 1024], P('row', 'col')
All inputs are finite; a program needn't handle non-finite values. No bound on the sum of `tile_mask` on one device may be relied on, other than what follows from the above.
Results may differ from a plain program's by a relative error of at most 0.001.
Values may be sent and summed in bfloat16 or wider, within the bound.
No kernel may reach another device: no remote copies, remote signals or barrier semaphores. Data moves between devices by JAX's collectives and lax.ppermute only.
A program may use at most 64 MiB of HBM per device.

v0:
```python
import functools

import jax
import jax.numpy as jnp
from jax import lax
from jax.experimental import pallas as pl
from jax.experimental.pallas import tpu as pltpu
from jax.sharding import PartitionSpec as P

TILE = 128
CODE_ROWS = 16
LEVELS = 32767.0
STEPS_PER_OCTAVE = 64.0
BLOCK_ROWS = 256
ADD_ROWS = 512


def apply_mask(amplitudes, tile_mask):
    tiles_m, tiles_k = tile_mask.shape
    tile_rows = amplitudes.shape[0] // tiles_m
    tile_cols = amplitudes.shape[1] // tiles_k
    blocks = amplitudes.reshape(tiles_m, tile_rows, tiles_k, tile_cols)
    weights = tile_mask.astype(amplitudes.dtype)[:, None, :, None]
    return (blocks * weights).reshape(amplitudes.shape)


def general(amplitudes, integrals, tile_mask):
    masked = apply_mask(amplitudes, tile_mask)
    partial_sums = jnp.dot(
        masked,
        lax.all_gather(integrals, "row", axis=1, tiled=True),
        preferred_element_type=jnp.float32,
    )
    summed = lax.psum_scatter(partial_sums, "col", scatter_dimension=1, tiled=True)
    return summed.astype(jnp.bfloat16)


def decode(ref, step, rows, block_rows, weight):
    groups = block_rows // TILE
    start = pl.multiple_of(step * block_rows, block_rows)
    levels = ref[pl.ds(start, block_rows), :].astype(jnp.int32).astype(jnp.float32)
    codes = ref[pl.ds(rows, CODE_ROWS), :].astype(jnp.int32).astype(jnp.float32)
    pieces = []
    which = lax.broadcasted_iota(jnp.int32, codes.shape, 0)
    for g in range(groups):
        code = jnp.sum(jnp.where(which == step * groups + g, codes, 0.0), axis=0, keepdims=True)
        unit = jnp.exp2(code / STEPS_PER_OCTAVE) * (weight / LEVELS)
        pieces.append(levels[g * TILE : (g + 1) * TILE] * unit)
    return jnp.concatenate(pieces, axis=0)


def encode(acc, step, out_ref, code_ref, rows):
    block_rows = acc.shape[0]
    groups = block_rows // TILE
    pieces = []
    for g in range(groups):
        part = acc[g * TILE : (g + 1) * TILE]
        largest = jnp.max(jnp.abs(part), axis=0, keepdims=True)
        code = jnp.ceil(jnp.log(jnp.maximum(largest, 1e-30)) * (STEPS_PER_OCTAVE / 0.6931471805599453))
        scaled = jnp.round(part * (jnp.exp2(-code / STEPS_PER_OCTAVE) * LEVELS))
        pieces.append(jnp.clip(scaled, -LEVELS, LEVELS).astype(jnp.int32))
        code_ref[pl.ds(step * groups + g, 1), :] = code
    start = pl.multiple_of(step * block_rows, block_rows)
    out_ref[pl.ds(start, block_rows), :] = jnp.concatenate(pieces, axis=0).astype(jnp.int16)

    @pl.when(step == pl.num_programs(0) - 1)
    def _():
        out_ref[pl.ds(rows, CODE_ROWS), :] = code_ref[...].astype(jnp.int32).astype(jnp.int16)


def fetch(chosen, core, whole, mine, other, b, columns, sem):
    half = b.shape[0] // 2

    @pl.when(chosen == 0)
    def _():
        pltpu.make_async_copy(whole, b.at[:, columns], sem).start()

    for j in range(3):

        @pl.when(chosen == j + 1)
        def _():
            here = pl.ds(pl.multiple_of(core * half, half), half)
            there = pl.ds(pl.multiple_of((1 - core) * half, half), half)
            pltpu.make_async_copy(mine[j], b.at[here, columns], sem).start()
            pltpu.make_async_copy(other[j], b.at[there, columns], sem).start()


def multiply_kernel(slots, kinds, rows, width, facts, a_ref, *refs):
    whole, mine, other, refs = refs[0], refs[1:4], refs[4:7], refs[7:]
    count = sum(len(kind) for kind in kinds)
    outs, refs = list(refs[:count]), refs[count:]
    b, sems, codes = refs[0], refs[1], list(refs[2:])
    step = pl.program_id(0)

    @pl.when(step == 0)
    def _():
        spans = [pl.ds(j * width, width) for j in range(len(slots))]
        for j, slot in enumerate(slots):
            fetch(facts[slot] ^ facts[CHIP], facts[CORE], whole, mine, other, b, spans[j], sems.at[j])
        for j, span in enumerate(spans):
            pltpu.make_async_copy(whole, b.at[:, span], sems.at[j]).wait()

    acc = jnp.dot(a_ref[...], b[...], preferred_element_type=jnp.float32)
    for j, kind in enumerate(kinds):
        part = acc[:, j * width : (j + 1) * width]
        for form in kind:
            out_ref = outs.pop(0)
            if form == "coded":
                encode(part, step, out_ref, codes.pop(0), rows)
            else:
                out_ref[...] = part


def multiply(facts, masked, columns, slots, kinds):
    rows, depth = masked.shape
    width = columns[0].shape[1]
    packed = (rows + CODE_ROWS, width)
    forms = [form for kind in kinds for form in kind]
    coded = (pl.BlockSpec(packed, lambda i, c: (0, 0)), jax.ShapeDtypeStruct(packed, jnp.int16))
    plain = (pl.BlockSpec((BLOCK_ROWS, width), lambda i, c: (i, 0)), jax.ShapeDtypeStruct((rows, width), jnp.float32))
    outs = [coded if form == "coded" else plain for form in forms]
    return pl.pallas_call(
        functools.partial(multiply_kernel, slots, kinds, rows, width),
        out_shape=[shape for _, shape in outs],
        grid_spec=pltpu.PrefetchScalarGridSpec(
            num_scalar_prefetch=1,
            grid=(rows // BLOCK_ROWS,),
            in_specs=[pl.BlockSpec((BLOCK_ROWS, depth), lambda i, c: (i, 0))]
            + [pl.BlockSpec(memory_space=pl.ANY)] * len(columns),
            out_specs=[spec for spec, _ in outs],
            scratch_shapes=[pltpu.VMEM((depth, width * len(slots)), masked.dtype), pltpu.SemaphoreType.DMA((4,))]
            + [pltpu.VMEM((CODE_ROWS, width), jnp.float32)] * forms.count("coded"),
        ),
        compiler_params=pltpu.CompilerParams(vmem_limit_bytes=24 * 1024 * 1024),
        cost_estimate=pl.CostEstimate(flops=3000000000, bytes_accessed=9000000, transcendentals=0),
    )(facts, masked, *columns)


def add_kernel(terms, beside, rows, facts, *refs):
    step = pl.program_id(0)
    blocks, refs = refs[: len(terms)], refs[len(terms) :]
    acc = None
    for block, weight in zip(blocks, terms):
        share = facts[weight].astype(jnp.float32)
        if block.dtype == jnp.int16:
            value = decode(block, step, rows, ADD_ROWS, share)
        else:
            value = block[...] if weight == ALWAYS else block[...] * share
        acc = value if acc is None else acc + value
    out_ref = refs[beside]
    if out_ref.dtype == jnp.int16:
        encode(acc, step, out_ref, refs[beside + 1], rows)
    else:
        acc = acc.astype(out_ref.dtype)
        out_ref[...] = jnp.concatenate([refs[0][...], acc], axis=1) if beside else acc


def add(facts, terms, dtype=jnp.int16, left=None):
    rows, width = next(x.shape for x, _ in terms if x.dtype == jnp.float32)
    packed = (rows + CODE_ROWS, width)
    beside = () if left is None else (left,)
    plain = pl.BlockSpec((ADD_ROWS, width), lambda i, c: (i, 0))
    coded = pl.BlockSpec(packed, lambda i, c: (0, 0))
    if dtype == jnp.int16:
        out_spec, out_shape = coded, jax.ShapeDtypeStruct(packed, dtype)
        scratch = [pltpu.VMEM((CODE_ROWS, width), jnp.float32)]
    else:
        total = width * (1 + len(beside))
        out_spec = pl.BlockSpec((ADD_ROWS, total), lambda i, c: (i, 0))
        out_shape = jax.ShapeDtypeStruct((rows, total), dtype)
        scratch = []
    return pl.pallas_call(
        functools.partial(add_kernel, tuple(weight for _, weight in terms), len(beside), rows),
        out_shape=out_shape,
        grid_spec=pltpu.PrefetchScalarGridSpec(
            num_scalar_prefetch=1,
            grid=(rows // ADD_ROWS,),
            in_specs=[coded if x.dtype == jnp.int16 else plain for x, _ in terms] + [plain] * len(beside),
            out_specs=out_spec,
            scratch_shapes=scratch,
        ),
        compiler_params=pltpu.CompilerParams(vmem_limit_bytes=16 * 1024 * 1024),
        cost_estimate=pl.CostEstimate(flops=3000000000, bytes_accessed=9000000, transcendentals=0),
    )(facts, *[x for x, _ in terms], *beside)


PLAN = (
    (3, 2, 1, 0, 1, 1, 0),
    (0, 2, 3, 1, 1, 0, 1),
    (3, 1, 0, 2, 1, 0, 1),
    (0, 1, 2, 3, 1, 1, 0),
)
FIRST, SECOND, THIRD, HERE, ALWAYS, OUTER, INNER, CORE, CHIP = range(9)


def line_of_four(amplitudes, integrals, tile_mask):
    row = lax.axis_index("row")
    core, chip = row % 2, row // 2
    half = integrals.shape[0] // 2

    def after(value, *others):
        return lax.optimization_barrier((value, *others))[0]

    def across(block, bit):
        return lax.ppermute(block, "row", [(i, i ^ bit) for i in range(8)])

    def choose(low, high):
        return jnp.where(core == 0, low, high)

    def along(block, pairs):
        return lax.ppermute(block, "col", pairs)

    twin = across(integrals, 1)
    mine_a = choose(integrals[:half], twin[half:])
    own, pair, tile_mask, plan = lax.optimization_barrier(
        (integrals, twin, tile_mask, jnp.asarray(PLAN, jnp.int32), mine_a)
    )[:4]
    masked = apply_mask(amplitudes, tile_mask)
    planned = lax.dynamic_slice_in_dim(plan, lax.axis_index("col"), 1)[0]
    facts = jnp.concatenate([planned, jnp.stack([core, chip]).astype(jnp.int32)])
    mine_b = choose(pair[:half], own[half:])
    own, pair = lax.optimization_barrier((own, pair, mine_b))[:2]
    whole_a, whole_b = choose(own, pair), choose(pair, own)

    got_a = [across(mine_a, bit) for bit in (2, 4, 6)]
    swapped_a = [across(after(x, masked, facts, whole_a, whole_b), 1) for x in got_a]
    columns_a = (whole_a, *got_a, *swapped_a)
    got_b = [across(after(mine_b, got_a[0]), bit) for bit in (2, 4, 6)]

    pairs = [(0, 1), (1, 0), (2, 3), (3, 2)]
    inward = [(0, 1), (3, 2)]
    jump = [(0, 1), (1, 3), (2, 0), (3, 2)]
    middle = [(1, 2), (2, 1)]
    coded, plain = ("coded",), ("plain",)
    (out_one,) = multiply(facts, masked, columns_a, (FIRST,), (coded,))
    one = along(out_one, pairs)
    out_two, second_a, third_a, here_a = multiply(
        after(facts, out_one), masked, columns_a, (SECOND, THIRD, HERE), (coded + plain, plain, plain)
    )
    two = along(out_two, inward)
    out_three = add(after(facts, out_two), [(third_a, ALWAYS), (one, INNER)])
    three = along(out_three, jump)
    out_near_a = add(after(facts, out_three), [(second_a, ALWAYS), (two, INNER)])
    near_a = along(out_near_a, middle)
    swapped_b = [across(after(x, out_two), 1) for x in got_b]
    columns_b = (whole_b, *got_b, *swapped_b)
    out_four, out_five, second_b = multiply(
        after(facts, out_near_a), masked, columns_b, (FIRST, SECOND), (coded, coded + plain)
    )
    four = along(out_four, pairs)
    five = along(out_five, inward)
    third_b, here_b = multiply(after(facts, out_five, three), masked, columns_b, (THIRD, HERE), (plain, plain))
    out_six = add(facts, [(third_b, ALWAYS), (four, INNER)])
    six = along(out_six, jump)
    out_near_b = add(after(facts, out_six, near_a), [(second_b, ALWAYS), (five, INNER)])
    near_b = along(out_near_b, middle)
    left = add(
        after(facts, out_near_b),
        [(here_a, ALWAYS), (one, OUTER), (three, ALWAYS), (near_a, INNER)],
        jnp.bfloat16,
    )
    most_b = add(after(facts, left), [(here_b, ALWAYS), (four, OUTER), (six, ALWAYS)], jnp.float32)
    return add(facts, [(most_b, ALWAYS), (near_b, INNER)], jnp.bfloat16, left)


def solution(mesh):
    body = line_of_four if mesh.shape["col"] == 4 and mesh.shape["row"] == 8 else general
    placed = (P("row", "col"), P("col", "row"), P("row", "col"))
    return jax.shard_map(
        body, mesh=mesh, in_specs=placed, out_specs=P("row", "col"), check_vma=False
    )
```

profile of v0, /device:TPU:10, one launch (start us, length us, event | category | flops | bytes accessed | tf_op | source)
XLA Modules:
  0.0 72.2 jit_solution(11225704509574552190)
XLA Ops:
  0.0 2.1 %collective-permute-done = bf16[2048,128]{1,0:T(8,128)(2,1)S(1)} collective-permute-done((bf16[2048,128]{1,0:T(8,128)(2,1)}, bf16[2048,128]{1,0:T(8,128)(2,1)S(1)}, u32[]{:S(2)}, u32[]{:S(2)}) %collective-permute-start) | collective-permute-done | bytes 524320 | tf_op jit(solution)/shard_map/ppermute | solution.py:205
  2.1 1.0 %slice_select_fusion = bf16[1024,128]{1,0:T(8,128)(2,1)S(1)} fusion(bf16[2048,128]{1,0:T(8,128)(2,1)S(1)} %collective-permute-done, bf16[2048,128]{1,0:T(8,128)(2,1)} %param.5, pred[]{:T(512)S(6)} %eq.4), kind=kLoop, calls=%fused_computation.3 | loop fusion | flops 131072 | bytes 786433 | tf_op jit(solution)/shard_map/jit(_where)/select_n | solution.py:208
  3.1 1.6 %collective-permute-start.3 = (bf16[1024,128]{1,0:T(8,128)(2,1)S(1)}, bf16[1024,128]{1,0:T(8,128)(2,1)S(1)}, u32[]{:S(2)}, u32[]{:S(2)}) collective-permute-start(bf16[1024,128]{1,0:T(8,128)(2,1)S(1)} %slice_select_fusion), channel_id=1, source_target_pairs={{0,24},{4,28},{8,16},{12,20},{16,8},{20,12},{24,0},{28,4},{1,25},{... | collective-permute-start | bytes 786440 | tf_op jit(solution)/shard_map/ppermute | solution.py:205
  4.7 0.5 collective-permute-start.2
  5.2 1.5 %collective-permute-start.1 = (bf16[1024,128]{1,0:T(8,128)(2,1)S(1)}, bf16[1024,128]{1,0:T(8,128)(2,1)S(1)}, u32[]{:S(2)}, u32[]{:S(2)}) collective-permute-start(bf16[1024,128]{1,0:T(8,128)(2,1)S(1)} %slice_select_fusion), channel_id=1, source_target_pairs={{0,8},{4,12},{8,0},{12,4},{16,24},{20,28},{24,16},{28,20},{1,9},{5... | collective-permute-start | bytes 786440 | tf_op jit(solution)/shard_map/ppermute | solution.py:205
  6.7 0.7 convert_element_type.3
  7.3 1.0 %slice_select_fusion.1 = bf16[1024,128]{1,0:T(8,128)(2,1)S(1)} fusion(bf16[2048,128]{1,0:T(8,128)(2,1)} %param.5, bf16[2048,128]{1,0:T(8,128)(2,1)S(1)} %collective-permute-done, pred[]{:T(512)S(6)} %eq.4), kind=kLoop, calls=%fused_computation.4 | loop fusion | flops 131072 | bytes 786433 | tf_op jit(solution)/shard_map/jit(_where)/select_n | solution.py:208
  8.3 0.6 mul.11
  9.0 0.9 %bitcast_multiply_fusion.a_ref = bf16[1024,2048]{1,0:T(8,128)(2,1)S(1)} fusion(bf16[1024,2048]{1,0:T(8,128)(2,1)S(1)} %copy-done, bf16[128,8,16,128]{3,2,1,0:T(8,128)(2,1)S(1)} %bitcast.8), kind=kLoop, calls=%fused_computation | loop fusion | flops 2097152 | bytes 12582912 | tf_op jit(solution)/shard_map/mul | solution.py:24
  9.9 0.1 copy-done.1
  10.0 0.1 broadcast_select_fusion
  10.1 0.7 dynamic-slice_bitcast_fusion
  10.8 0.1 pad_add_fusion.facts
  10.8 2.4 %collective-permute-done.3.refs_3_ = bf16[1024,128]{1,0:T(8,128)(2,1)S(1)} collective-permute-done((bf16[1024,128]{1,0:T(8,128)(2,1)S(1)}, bf16[1024,128]{1,0:T(8,128)(2,1)S(1)}, u32[]{:S(2)}, u32[]{:S(2)}) %collective-permute-start.3) | collective-permute-done | bytes 262176 | tf_op jit(solution)/shard_map/ppermute | solution.py:205
  13.3 4.8 %collective-permute-done.2.refs_2_ = bf16[1024,128]{1,0:T(8,128)(2,1)S(1)} collective-permute-done((bf16[1024,128]{1,0:T(8,128)(2,1)S(1)}, bf16[1024,128]{1,0:T(8,128)(2,1)S(1)}, u32[]{:S(2)}, u32[]{:S(2)}) %collective-permute-start.2) | collective-permute-done | bytes 262176 | tf_op jit(solution)/shard_map/ppermute | solution.py:205
  18.0 0.0 collective-permute-start.5
  18.1 0.1 collective-permute-done.1.refs_1_
  18.1 0.4 collective-permute-start.4
  18.5 1.5 %collective-permute-start.11 = (bf16[1024,128]{1,0:T(8,128)(2,1)S(1)}, bf16[1024,128]{1,0:T(8,128)(2,1)S(1)}, u32[]{:S(2)}, u32[]{:S(2)}) collective-permute-start(bf16[1024,128]{1,0:T(8,128)(2,1)S(1)} %slice_select_fusion.1), channel_id=1, source_target_pairs={{0,24},{4,28},{8,16},{12,20},{16,8},{20,12},{24,0},{28,4},{1,25},{... | collective-permute-start | bytes 786440 | tf_op jit(solution)/shard_map/ppermute | solution.py:205
  20.0 0.5 collective-permute-start.10
  20.6 1.5 %collective-permute-start.9 = (bf16[1024,128]{1,0:T(8,128)(2,1)S(1)}, bf16[1024,128]{1,0:T(8,128)(2,1)S(1)}, u32[]{:S(2)}, u32[]{:S(2)}) collective-permute-start(bf16[1024,128]{1,0:T(8,128)(2,1)S(1)} %slice_select_fusion.1), channel_id=1, source_target_pairs={{0,8},{4,12},{8,0},{12,4},{16,24},{20,28},{24,16},{28,20},{1,9},{5... | collective-permute-start | bytes 786440 | tf_op jit(solution)/shard_map/ppermute | solution.py:205
  22.0 2.6 %shard_map.46 = s16[1040,128]{1,0:T(8,128)(2,1)S(1)} custom-call(s32[9]{0:T(128)S(1)} %pad_add_fusion.facts, bf16[1024,2048]{1,0:T(8,128)(2,1)S(1)} %bitcast_multiply_fusion.a_ref, bf16[2048,128]{1,0:T(8,128)(2,1)S(1)} %get-tuple-element.66.refs_0_, bf16[1024,128]{1,0:T(8,128)(2,1)S(1)} %collective-permute-done.1.refs_1_, ...), custom_call_target="tpu_custom_call" | custom-call | flops 3000000000 | bytes 9000000 | tf_op jit(solution)/shard_map/pallas_call | solution.py:122
  24.6 0.5 collective-permute-start.7
  25.2 4.1 %shard_map.47 = (s16[1040,128]{1,0:T(8,128)(2,1)S(1)}, f32[1024,128]{1,0:T(8,128)S(1)}, f32[1024,128]{1,0:T(8,128)S(1)}, f32[1024,128]{1,0:T(8,128)S(1)}) custom-call(s32[9]{0:T(128)S(1)} %pad_add_fusion.facts, bf16[1024,2048]{1,0:T(8,128)(2,1)S(1)} %bitcast_multiply_fusion.a_ref, bf16[2048,128]{1,0:T(8,128)(2,1)S(1)} %get-tuple-element.66.refs_0_, ...), custom_call_target="tpu_custom_call" | custom-call | flops 3000000000 | bytes 9000000 | tf_op jit(solution)/shard_map/pallas_call | solution.py:122
  29.3 1.3 %collective-permute-start.8 = (s16[1040,128]{1,0:T(8,128)(2,1)S(1)}, s16[1040,128]{1,0:T(8,128)(2,1)S(1)}, u32[]{:S(2)}, u32[]{:S(2)}) collective-permute-start(s16[1040,128]{1,0:T(8,128)(2,1)S(1)} %get-tuple-element.45), channel_id=1, source_target_pairs={{0,1},{3,2},{4,5},{7,6},{8,9},{11,10},{12,13},{15,14},{16,17},{19,... | collective-permute-start | bytes 798728 | tf_op jit(solution)/shard_map/ppermute | solution.py:211
  30.6 0.1 collective-permute-start.14
  30.6 2.7 %collective-permute-done.10.refs_2_ = bf16[1024,128]{1,0:T(8,128)(2,1)S(1)} collective-permute-done((bf16[1024,128]{1,0:T(8,128)(2,1)S(1)}, bf16[1024,128]{1,0:T(8,128)(2,1)S(1)}, u32[]{:S(2)}, u32[]{:S(2)}) %collective-permute-start.10) | collective-permute-done | bytes 262176 | tf_op jit(solution)/shard_map/ppermute | solution.py:205
  33.4 0.0 collective-permute-start.13
  33.4 0.5 collective-permute-start.12
  33.9 0.8 %shard_map.48 = s16[1040,128]{1,0:T(8,128)(2,1)S(1)} custom-call(s32[9]{0:T(128)S(1)} %pad_add_fusion.facts, f32[1024,128]{1,0:T(8,128)S(1)} %get-tuple-element.47.refs_0_, s16[1040,128]{1,0:T(8,128)(2,1)S(1)} %collective-permute-done.7.refs_1_), custom_call_target="tpu_custom_call" | custom-call | flops 3000000000 | bytes 9000000 | tf_op jit(solution)/shard_map/pallas_call | solution.py:172
  34.7 2.6 %collective-permute-start.15 = (s16[1040,128]{1,0:T(8,128)(2,1)S(1)}, s16[1040,128]{1,0:T(8,128)(2,1)S(1)}, u32[]{:S(2)}, u32[]{:S(2)}) collective-permute-start(s16[1040,128]{1,0:T(8,128)(2,1)S(1)} %shard_map.48), channel_id=1, source_target_pairs={{0,1},{1,3},{2,0},{3,2},{4,5},{5,7},{6,4},{7,6},{8,9},{9,11},{10,8... | collective-permute-start | bytes 798728 | tf_op jit(solution)/shard_map/ppermute | solution.py:211
  37.3 2.1 %collective-permute-done.8.refs_1_ = s16[1040,128]{1,0:T(8,128)(2,1)S(1)} collective-permute-done((s16[1040,128]{1,0:T(8,128)(2,1)S(1)}, s16[1040,128]{1,0:T(8,128)(2,1)S(1)}, u32[]{:S(2)}, u32[]{:S(2)}) %collective-permute-start.8) | collective-permute-done | bytes 266272 | tf_op jit(solution)/shard_map/ppermute | solution.py:211
  39.4 0.8 %shard_map.49 = s16[1040,128]{1,0:T(8,128)(2,1)S(1)} custom-call(s32[9]{0:T(128)S(1)} %pad_add_fusion.facts, f32[1024,128]{1,0:T(8,128)S(1)} %get-tuple-element.49.refs_0_, s16[1040,128]{1,0:T(8,128)(2,1)S(1)} %collective-permute-done.8.refs_1_), custom_call_target="tpu_custom_call" | custom-call | flops 3000000000 | bytes 9000000 | tf_op jit(solution)/shard_map/pallas_call | solution.py:172
  40.2 5.7 %collective-permute-start.17 = (s16[1040,128]{1,0:T(8,128)(2,1)S(1)}, s16[1040,128]{1,0:T(8,128)(2,1)S(1)}, u32[]{:S(2)}, u32[]{:S(2)}) collective-permute-start(s16[1040,128]{1,0:T(8,128)(2,1)S(1)} %shard_map.49), channel_id=1, source_target_pairs={{1,2},{2,1},{5,6},{6,5},{9,10},{10,9},{13,14},{14,13},{17,18},{18,... | collective-permute-start | bytes 798728 | tf_op jit(solution)/shard_map/ppermute | solution.py:211
  45.9 3.1 %shard_map.50 = (s16[1040,128]{1,0:T(8,128)(2,1)S(1)}, s16[1040,128]{1,0:T(8,128)(2,1)S(1)}, f32[1024,128]{1,0:T(8,128)S(1)}) custom-call(s32[9]{0:T(128)S(1)} %pad_add_fusion.facts, bf16[1024,2048]{1,0:T(8,128)(2,1)S(1)} %bitcast_multiply_fusion.a_ref, bf16[2048,128]{1,0:T(8,128)(2,1)S(1)} %get-tuple-element.65.refs_0_, ...), custom_call_target="tpu_custom_call" | custom-call | flops 3000000000 | bytes 9000000 | tf_op jit(solution)/shard_map/pallas_call | solution.py:122
  49.0 0.1 collective-permute-start.16
  49.1 1.3 %collective-permute-start.18 = (s16[1040,128]{1,0:T(8,128)(2,1)S(1)}, s16[1040,128]{1,0:T(8,128)(2,1)S(1)}, u32[]{:S(2)}, u32[]{:S(2)}) collective-permute-start(s16[1040,128]{1,0:T(8,128)(2,1)S(1)} %get-tuple-element.55), channel_id=1, source_target_pairs={{0,1},{3,2},{4,5},{7,6},{8,9},{11,10},{12,13},{15,14},{16,17},{19,... | collective-permute-start | bytes 798728 | tf_op jit(solution)/shard_map/ppermute | solution.py:211
  50.4 2.7 %shard_map.51 = (f32[1024,128]{1,0:T(8,128)S(1)}, f32[1024,128]{1,0:T(8,128)S(1)}) custom-call(s32[9]{0:T(128)S(1)} %pad_add_fusion.facts, bf16[1024,2048]{1,0:T(8,128)(2,1)S(1)} %bitcast_multiply_fusion.a_ref, bf16[2048,128]{1,0:T(8,128)(2,1)S(1)} %get-tuple-element.65.refs_0_, bf16[1024,128]{1,0:T(8,128)(2,1)S(1)} %collective-permute-done.9.refs_1_, ...), custom_call_target="tpu_custom_call" | custom-call | flops 3000000000 | bytes 9000000 | tf_op jit(solution)/shard_map/pallas_call | solution.py:122
  53.1 5.0 %collective-permute-done.16.refs_1_ = s16[1040,128]{1,0:T(8,128)(2,1)S(1)} collective-permute-done((s16[1040,128]{1,0:T(8,128)(2,1)S(1)}, s16[1040,128]{1,0:T(8,128)(2,1)S(1)}, u32[]{:S(2)}, u32[]{:S(2)}) %collective-permute-start.16) | collective-permute-done | bytes 266272 | tf_op jit(solution)/shard_map/ppermute | solution.py:211
  58.1 0.8 %shard_map.52 = s16[1040,128]{1,0:T(8,128)(2,1)S(1)} custom-call(s32[9]{0:T(128)S(1)} %pad_add_fusion.facts, f32[1024,128]{1,0:T(8,128)S(1)} %get-tuple-element.57.refs_0_, s16[1040,128]{1,0:T(8,128)(2,1)S(1)} %collective-permute-done.16.refs_1_), custom_call_target="tpu_custom_call" | custom-call | flops 3000000000 | bytes 9000000 | tf_op jit(solution)/shard_map/pallas_call | solution.py:172
  58.9 0.1 collective-permute-start.19
  59.0 2.7 %collective-permute-done.18.refs_1_ = s16[1040,128]{1,0:T(8,128)(2,1)S(1)} collective-permute-done((s16[1040,128]{1,0:T(8,128)(2,1)S(1)}, s16[1040,128]{1,0:T(8,128)(2,1)S(1)}, u32[]{:S(2)}, u32[]{:S(2)}) %collective-permute-start.18) | collective-permute-done | bytes 266272 | tf_op jit(solution)/shard_map/ppermute | solution.py:211
  61.7 0.8 %shard_map.53 = s16[1040,128]{1,0:T(8,128)(2,1)S(1)} custom-call(s32[9]{0:T(128)S(1)} %pad_add_fusion.facts, f32[1024,128]{1,0:T(8,128)S(1)} %get-tuple-element.60.refs_0_, s16[1040,128]{1,0:T(8,128)(2,1)S(1)} %collective-permute-done.18.refs_1_), custom_call_target="tpu_custom_call" | custom-call | flops 3000000000 | bytes 9000000 | tf_op jit(solution)/shard_map/pallas_call | solution.py:172
  62.5 2.2 %collective-permute-start.20 = (s16[1040,128]{1,0:T(8,128)(2,1)S(1)}, s16[1040,128]{1,0:T(8,128)(2,1)S(1)}, u32[]{:S(2)}, u32[]{:S(2)}) collective-permute-start(s16[1040,128]{1,0:T(8,128)(2,1)S(1)} %shard_map.53), channel_id=1, source_target_pairs={{1,2},{2,1},{5,6},{6,5},{9,10},{10,9},{13,14},{14,13},{17,18},{18,... | collective-permute-start | bytes 798728 | tf_op jit(solution)/shard_map/ppermute | solution.py:211
  64.7 0.9 %shard_map.54.refs_2_ = bf16[1024,128]{1,0:T(8,128)(2,1)S(1)} custom-call(s32[9]{0:T(128)S(1)} %pad_add_fusion.facts, f32[1024,128]{1,0:T(8,128)S(1)} %get-tuple-element.62.refs_0_, s16[1040,128]{1,0:T(8,128)(2,1)S(1)} %collective-permute-done.7.refs_1_, s16[1040,128]{1,0:T(8,128)(2,1)S(1)} %collective-permute-done.15.refs_2_, ...), custom_call_target="tpu_custom_call" | custom-call | flops 3000000000 | bytes 9000000 | tf_op jit(solution)/shard_map/pallas_call | solution.py:172
  65.6 0.8 %shard_map.55.refs_0_ = f32[1024,128]{1,0:T(8,128)S(1)} custom-call(s32[9]{0:T(128)S(1)} %pad_add_fusion.facts, f32[1024,128]{1,0:T(8,128)S(1)} %get-tuple-element.64.refs_0_, s16[1040,128]{1,0:T(8,128)(2,1)S(1)} %collective-permute-done.16.refs_1_, s16[1040,128]{1,0:T(8,128)(2,1)S(1)} %collective-permute-done.19.refs_2_), custom_call_target="tpu_custom_call" | custom-call | flops 3000000000 | bytes 9000000 | tf_op jit(solution)/shard_map/pallas_call | solution.py:172
  66.3 4.5 %collective-permute-done.20.refs_1_ = s16[1040,128]{1,0:T(8,128)(2,1)S(1)} collective-permute-done((s16[1040,128]{1,0:T(8,128)(2,1)S(1)}, s16[1040,128]{1,0:T(8,128)(2,1)S(1)}, u32[]{:S(2)}, u32[]{:S(2)}) %collective-permute-start.20) | collective-permute-done | bytes 266272 | tf_op jit(solution)/shard_map/ppermute | solution.py:211
  70.8 1.4 %shard_map.56 = bf16[1024,256]{1,0:T(8,128)(2,1)} custom-call(s32[9]{0:T(128)S(1)} %pad_add_fusion.facts, f32[1024,128]{1,0:T(8,128)S(1)} %shard_map.55.refs_0_, s16[1040,128]{1,0:T(8,128)(2,1)S(1)} %collective-permute-done.20.refs_1_, bf16[1024,128]{1,0:T(8,128)(2,1)S(1)} %shard_map.54.refs_2_), custom_call_target="tpu_custom_call" | custom-call | flops 3000000000 | bytes 9000000 | tf_op jit(solution)/shard_map/pallas_call | solution.py:172
  (17 shorter events, 0.0 us)
Async XLA Ops:
  0.0 2.1 %collective-permute-start = (bf16[2048,128]{1,0:T(8,128)(2,1)}, bf16[2048,128]{1,0:T(8,128)(2,1)S(1)}, u32[]{:S(2)}, u32[]{:S(2)}) collective-permute-start(bf16[2048,128]{1,0:T(8,128)(2,1)} %param.5), channel_id=1, source_target_pairs={{0,4},{4,0},{8,12},{12,8},{16,20},{20,16},{24,28},{28,24},{1,5},{5... | collective-permute-start | bytes 1572872 | tf_op jit(solution)/shard_map/ppermute | solution.py:205
  0.0 8.9 %copy-start = (bf16[1024,2048]{1,0:T(8,128)(2,1)S(1)}, bf16[1024,2048]{1,0:T(8,128)(2,1)}, u32[]{:S(2)}) copy-start(bf16[1024,2048]{1,0:T(8,128)(2,1)} %param.4) | copy-start | bytes 12582916
  3.1 10.2 %collective-permute-start.3 = (bf16[1024,128]{1,0:T(8,128)(2,1)S(1)}, bf16[1024,128]{1,0:T(8,128)(2,1)S(1)}, u32[]{:S(2)}, u32[]{:S(2)}) collective-permute-start(bf16[1024,128]{1,0:T(8,128)(2,1)S(1)} %slice_select_fusion), channel_id=1, source_target_pairs={{0,24},{4,28},{8,16},{12,20},{16,8},{20,12},{24,0},{28,4},{1,25},{... | collective-permute-start | bytes 786440 | tf_op jit(solution)/shard_map/ppermute | solution.py:205
  4.7 13.4 %collective-permute-start.2 = (bf16[1024,128]{1,0:T(8,128)(2,1)S(1)}, bf16[1024,128]{1,0:T(8,128)(2,1)S(1)}, u32[]{:S(2)}, u32[]{:S(2)}) collective-permute-start(bf16[1024,128]{1,0:T(8,128)(2,1)S(1)} %slice_select_fusion), channel_id=1, source_target_pairs={{0,16},{4,20},{8,24},{12,28},{16,0},{20,4},{24,8},{28,12},{1,17},{... | collective-permute-start | bytes 786440 | tf_op jit(solution)/shard_map/ppermute | solution.py:205
  5.2 13.0 %collective-permute-start.1 = (bf16[1024,128]{1,0:T(8,128)(2,1)S(1)}, bf16[1024,128]{1,0:T(8,128)(2,1)S(1)}, u32[]{:S(2)}, u32[]{:S(2)}) collective-permute-start(bf16[1024,128]{1,0:T(8,128)(2,1)S(1)} %slice_select_fusion), channel_id=1, source_target_pairs={{0,8},{4,12},{8,0},{12,4},{16,24},{20,28},{24,16},{28,20},{1,9},{5... | collective-permute-start | bytes 786440 | tf_op jit(solution)/shard_map/ppermute | solution.py:205
  9.0 1.0 %copy-start.1 = (bf16[2048,128]{1,0:T(8,128)(2,1)S(1)}, bf16[2048,128]{1,0:T(8,128)(2,1)}, u32[]{:S(2)}) copy-start(bf16[2048,128]{1,0:T(8,128)(2,1)} %param.5) | copy-start | bytes 1572868
  13.3 7.3 %collective-permute-start.6 = (bf16[1024,128]{1,0:T(8,128)(2,1)S(1)}, bf16[1024,128]{1,0:T(8,128)(2,1)S(1)}, u32[]{:S(2)}, u32[]{:S(2)}) collective-permute-start(bf16[1024,128]{1,0:T(8,128)(2,1)S(1)} %collective-permute-done.3.refs_3_), channel_id=1, source_target_pairs={{0,4},{4,0},{8,12},{12,8},{16,20},{20,16},{24,28},{28,24},{1,5},{5... | collective-permute-start | bytes 786440 | tf_op jit(solution)/shard_map/ppermute | solution.py:205
  18.0 4.0 %collective-permute-start.5 = (bf16[1024,128]{1,0:T(8,128)(2,1)S(1)}, bf16[1024,128]{1,0:T(8,128)(2,1)S(1)}, u32[]{:S(2)}, u32[]{:S(2)}) collective-permute-start(bf16[1024,128]{1,0:T(8,128)(2,1)S(1)} %collective-permute-done.2.refs_2_), channel_id=1, source_target_pairs={{0,4},{4,0},{8,12},{12,8},{16,20},{20,16},{24,28},{28,24},{1,5},{5... | collective-permute-start | bytes 786440 | tf_op jit(solution)/shard_map/ppermute | solution.py:205
  18.1 3.9 %collective-permute-start.4 = (bf16[1024,128]{1,0:T(8,128)(2,1)S(1)}, bf16[1024,128]{1,0:T(8,128)(2,1)S(1)}, u32[]{:S(2)}, u32[]{:S(2)}) collective-permute-start(bf16[1024,128]{1,0:T(8,128)(2,1)S(1)} %collective-permute-done.1.refs_1_), channel_id=1, source_target_pairs={{0,4},{4,0},{8,12},{12,8},{16,20},{20,16},{24,28},{28,24},{1,5},{5... | collective-permute-start | bytes 786440 | tf_op jit(solution)/shard_map/ppermute | solution.py:205
  18.5 12.0 %collective-permute-start.11 = (bf16[1024,128]{1,0:T(8,128)(2,1)S(1)}, bf16[1024,128]{1,0:T(8,128)(2,1)S(1)}, u32[]{:S(2)}, u32[]{:S(2)}) collective-permute-start(bf16[1024,128]{1,0:T(8,128)(2,1)S(1)} %slice_select_fusion.1), channel_id=1, source_target_pairs={{0,24},{4,28},{8,16},{12,20},{16,8},{20,12},{24,0},{28,4},{1,25},{... | collective-permute-start | bytes 786440 | tf_op jit(solution)/shard_map/ppermute | solution.py:205
  20.0 13.3 %collective-permute-start.10 = (bf16[1024,128]{1,0:T(8,128)(2,1)S(1)}, bf16[1024,128]{1,0:T(8,128)(2,1)S(1)}, u32[]{:S(2)}, u32[]{:S(2)}) collective-permute-start(bf16[1024,128]{1,0:T(8,128)(2,1)S(1)} %slice_select_fusion.1), channel_id=1, source_target_pairs={{0,16},{4,20},{8,24},{12,28},{16,0},{20,4},{24,8},{28,12},{1,17},{... | collective-permute-start | bytes 786440 | tf_op jit(solution)/shard_map/ppermute | solution.py:205
  20.6 12.8 %collective-permute-start.9 = (bf16[1024,128]{1,0:T(8,128)(2,1)S(1)}, bf16[1024,128]{1,0:T(8,128)(2,1)S(1)}, u32[]{:S(2)}, u32[]{:S(2)}) collective-permute-start(bf16[1024,128]{1,0:T(8,128)(2,1)S(1)} %slice_select_fusion.1), channel_id=1, source_target_pairs={{0,8},{4,12},{8,0},{12,4},{16,24},{20,28},{24,16},{28,20},{1,9},{5... | collective-permute-start | bytes 786440 | tf_op jit(solution)/shard_map/ppermute | solution.py:205
  24.6 9.3 %collective-permute-start.7 = (s16[1040,128]{1,0:T(8,128)(2,1)S(1)}, s16[1040,128]{1,0:T(8,128)(2,1)S(1)}, u32[]{:S(2)}, u32[]{:S(2)}) collective-permute-start(s16[1040,128]{1,0:T(8,128)(2,1)S(1)} %shard_map.46), channel_id=1, source_target_pairs={{0,1},{1,0},{2,3},{3,2},{4,5},{5,4},{6,7},{7,6},{8,9},{9,8},{10,11... | collective-permute-start | bytes 798728 | tf_op jit(solution)/shard_map/ppermute | solution.py:211
  29.3 10.1 %collective-permute-start.8 = (s16[1040,128]{1,0:T(8,128)(2,1)S(1)}, s16[1040,128]{1,0:T(8,128)(2,1)S(1)}, u32[]{:S(2)}, u32[]{:S(2)}) collective-permute-start(s16[1040,128]{1,0:T(8,128)(2,1)S(1)} %get-tuple-element.45), channel_id=1, source_target_pairs={{0,1},{3,2},{4,5},{7,6},{8,9},{11,10},{12,13},{15,14},{16,17},{19,... | collective-permute-start | bytes 798728 | tf_op jit(solution)/shard_map/ppermute | solution.py:211
  30.6 15.3 %collective-permute-start.14 = (bf16[1024,128]{1,0:T(8,128)(2,1)S(1)}, bf16[1024,128]{1,0:T(8,128)(2,1)S(1)}, u32[]{:S(2)}, u32[]{:S(2)}) collective-permute-start(bf16[1024,128]{1,0:T(8,128)(2,1)S(1)} %collective-permute-done.11.refs_3_), channel_id=1, source_target_pairs={{0,4},{4,0},{8,12},{12,8},{16,20},{20,16},{24,28},{28,24},{1,5},{5... | collective-permute-start | bytes 786440 | tf_op jit(solution)/shard_map/ppermute | solution.py:205
  33.4 12.5 %collective-permute-start.13 = (bf16[1024,128]{1,0:T(8,128)(2,1)S(1)}, bf16[1024,128]{1,0:T(8,128)(2,1)S(1)}, u32[]{:S(2)}, u32[]{:S(2)}) collective-permute-start(bf16[1024,128]{1,0:T(8,128)(2,1)S(1)} %collective-permute-done.10.refs_2_), channel_id=1, source_target_pairs={{0,4},{4,0},{8,12},{12,8},{16,20},{20,16},{24,28},{28,24},{1,5},{5... | collective-permute-start | bytes 786440 | tf_op jit(solution)/shard_map/ppermute | solution.py:205
  33.4 12.5 %collective-permute-start.12 = (bf16[1024,128]{1,0:T(8,128)(2,1)S(1)}, bf16[1024,128]{1,0:T(8,128)(2,1)S(1)}, u32[]{:S(2)}, u32[]{:S(2)}) collective-permute-start(bf16[1024,128]{1,0:T(8,128)(2,1)S(1)} %collective-permute-done.9.refs_1_), channel_id=1, source_target_pairs={{0,4},{4,0},{8,12},{12,8},{16,20},{20,16},{24,28},{28,24},{1,5},{5... | collective-permute-start | bytes 786440 | tf_op jit(solution)/shard_map/ppermute | solution.py:205
  34.7 15.7 %collective-permute-start.15 = (s16[1040,128]{1,0:T(8,128)(2,1)S(1)}, s16[1040,128]{1,0:T(8,128)(2,1)S(1)}, u32[]{:S(2)}, u32[]{:S(2)}) collective-permute-start(s16[1040,128]{1,0:T(8,128)(2,1)S(1)} %shard_map.48), channel_id=1, source_target_pairs={{0,1},{1,3},{2,0},{3,2},{4,5},{5,7},{6,4},{7,6},{8,9},{9,11},{10,8... | collective-permute-start | bytes 798728 | tf_op jit(solution)/shard_map/ppermute | solution.py:211
  40.2 18.7 %collective-permute-start.17 = (s16[1040,128]{1,0:T(8,128)(2,1)S(1)}, s16[1040,128]{1,0:T(8,128)(2,1)S(1)}, u32[]{:S(2)}, u32[]{:S(2)}) collective-permute-start(s16[1040,128]{1,0:T(8,128)(2,1)S(1)} %shard_map.49), channel_id=1, source_target_pairs={{1,2},{2,1},{5,6},{6,5},{9,10},{10,9},{13,14},{14,13},{17,18},{18,... | collective-permute-start | bytes 798728 | tf_op jit(solution)/shard_map/ppermute | solution.py:211
  49.0 9.1 %collective-permute-start.16 = (s16[1040,128]{1,0:T(8,128)(2,1)S(1)}, s16[1040,128]{1,0:T(8,128)(2,1)S(1)}, u32[]{:S(2)}, u32[]{:S(2)}) collective-permute-start(s16[1040,128]{1,0:T(8,128)(2,1)S(1)} %get-tuple-element.58), channel_id=1, source_target_pairs={{0,1},{1,0},{2,3},{3,2},{4,5},{5,4},{6,7},{7,6},{8,9},{9,8},{10,11... | collective-permute-start | bytes 798728 | tf_op jit(solution)/shard_map/ppermute | solution.py:211
  49.1 12.6 %collective-permute-start.18 = (s16[1040,128]{1,0:T(8,128)(2,1)S(1)}, s16[1040,128]{1,0:T(8,128)(2,1)S(1)}, u32[]{:S(2)}, u32[]{:S(2)}) collective-permute-start(s16[1040,128]{1,0:T(8,128)(2,1)S(1)} %get-tuple-element.55), channel_id=1, source_target_pairs={{0,1},{3,2},{4,5},{7,6},{8,9},{11,10},{12,13},{15,14},{16,17},{19,... | collective-permute-start | bytes 798728 | tf_op jit(solution)/shard_map/ppermute | solution.py:211
  58.9 6.7 %collective-permute-start.19 = (s16[1040,128]{1,0:T(8,128)(2,1)S(1)}, s16[1040,128]{1,0:T(8,128)(2,1)S(1)}, u32[]{:S(2)}, u32[]{:S(2)}) collective-permute-start(s16[1040,128]{1,0:T(8,128)(2,1)S(1)} %shard_map.52), channel_id=1, source_target_pairs={{0,1},{1,3},{2,0},{3,2},{4,5},{5,7},{6,4},{7,6},{8,9},{9,11},{10,8... | collective-permute-start | bytes 798728 | tf_op jit(solution)/shard_map/ppermute | solution.py:211
  62.5 8.3 %collective-permute-start.20 = (s16[1040,128]{1,0:T(8,128)(2,1)S(1)}, s16[1040,128]{1,0:T(8,128)(2,1)S(1)}, u32[]{:S(2)}, u32[]{:S(2)}) collective-permute-start(s16[1040,128]{1,0:T(8,128)(2,1)S(1)} %shard_map.53), channel_id=1, source_target_pairs={{1,2},{2,1},{5,6},{6,5},{9,10},{10,9},{13,14},{14,13},{17,18},{18,... | collective-permute-start | bytes 798728 | tf_op jit(solution)/shard_map/ppermute | solution.py:211
where the time goes:
time: 72.5 us; the launch traced here: 72.2 us
  waiting for transfers between devices  26.4 us (36%)
  starting transfers between devices  21.8 us (30%)
  Pallas kernels  18.7 us (26%)
  other arithmetic  3.7 us (5%)
  local copies, waits for them, and re-layouts  1.43 us (2%)
    ppermute x8, waiting for transfers between devices, along(): return lax.ppermute(block, 'col', pairs)  14.2 us
    ppermute x8, starting transfers between devices, along(): return lax.ppermute(block, 'col', pairs)  13.8 us
    pallas_call x4, Pallas kernels, multiply(): pl.pallas_call(functools.partial(multiply_kernel, slots, kinds, rows, wid...  12.4 us
    ppermute x13, waiting for transfers between devices, across(): return lax.ppermute(block, 'row', [(i, i ^ bit) for i in range(8)])  12.1 us
    ppermute x13, starting transfers between devices, across(): return lax.ppermute(block, 'row', [(i, i ^ bit) for i in range(8)])  8.06 us
    pallas_call x7, Pallas kernels, add(): pl.pallas_call(functools.partial(add_kernel, tuple((weight for _, weight...  6.23 us
    select_n x3, other arithmetic, choose(): return jnp.where(core == 0, low, high)  2.03 us
  transfers between devices with their start and end apart: 21, of which 9 were waited for; matrix products, arithmetic and copies ran while one was open for 6% of the time, Pallas kernels for 24%

commit v1 on v0

--- a/solution.py
+++ b/solution.py
@@ -11,7 +11,7 @@
 CODE_ROWS = 16
 LEVELS = 32767.0
 STEPS_PER_OCTAVE = 64.0
-BLOCK_ROWS = 256
+BLOCK_ROWS = 512
 ADD_ROWS = 512
 
 
@@ -234,22 +234,20 @@
     coded, plain = ("coded",), ("plain",)
     (out_one,) = multiply(facts, masked, columns_a, (FIRST,), (coded,))
     one = along(out_one, pairs)
-    out_two, second_a, third_a, here_a = multiply(
-        after(facts, out_one), masked, columns_a, (SECOND, THIRD, HERE), (coded + plain, plain, plain)
-    )
-    two = along(out_two, inward)
-    out_three = add(after(facts, out_two), [(third_a, ALWAYS), (one, INNER)])
+    out_two, second_a = multiply(after(facts, out_one), masked, columns_a, (SECOND,), (coded + plain,))
+    two = along(out_two, pairs)
+    third_a, here_a = multiply(after(facts, out_two), masked, columns_a, (THIRD, HERE), (plain, plain))
+    out_three = add(facts, [(third_a, ALWAYS), (one, INNER)])
     three = along(out_three, jump)
-    out_near_a = add(after(facts, out_three), [(second_a, ALWAYS), (two, INNER)])
+    swapped_b = [across(after(x, third_a), 1) for x in got_b]
+    columns_b = (whole_b, *got_b, *swapped_b)
+    (out_four,) = multiply(after(facts, out_three), masked, columns_b, (FIRST,), (coded,))
+    four = along(out_four, pairs)
+    out_five, second_b = multiply(after(facts, out_four), masked, columns_b, (SECOND,), (coded + plain,))
+    five = along(out_five, inward)
+    out_near_a = add(after(facts, out_five), [(second_a, ALWAYS), (two, INNER)])
     near_a = along(out_near_a, middle)
-    swapped_b = [across(after(x, out_two), 1) for x in got_b]
-    columns_b = (whole_b, *got_b, *swapped_b)
-    out_four, out_five, second_b = multiply(
-        after(facts, out_near_a), masked, columns_b, (FIRST, SECOND), (coded, coded + plain)
-    )
-    four = along(out_four, pairs)
-    five = along(out_five, inward)
-    third_b, here_b = multiply(after(facts, out_five, three), masked, columns_b, (THIRD, HERE), (plain, plain))
+    third_b, here_b = multiply(after(facts, out_near_a, three), masked, columns_b, (THIRD, HERE), (plain, plain))
     out_six = add(facts, [(third_b, ALWAYS), (four, INNER)])
     six = along(out_six, jump)
     out_near_b = add(after(facts, out_six, near_a), [(second_b, ALWAYS), (five, INNER)])

time: 72.5 us -> 67.3 us (0.928)
  waiting for transfers between devices: 26.4 us -> 18.4 us
  starting transfers between devices: 21.8 us -> 23.3 us
  Pallas kernels: 18.7 us -> 19.7 us
    ppermute x8, waiting for transfers between devices: 14.2 us -> 6.7 us  [along(): return lax.ppermute(block, 'col', pairs)]
    ppermute x8, starting transfers between devices: 13.8 us -> 15.2 us  [along(): return lax.ppermute(block, 'col', pairs)]
    pallas_call x4 -> x6, Pallas kernels: 12.4 us -> 13.4 us  [multiply(): pl.pallas_call(functools.partial(multiply_kernel, slots, kinds, rows, wid...]
  transfers between devices with their start and end apart: 21 -> 21, of which waited for: 9 -> 9; matrix products, arithmetic and copies ran while one was open for 6% -> 6% of each run, Pallas kernels for 24% -> 27%
where the time goes in v1:
time: 67.3 us; the launch traced here: 66.8 us
  starting transfers between devices  23.3 us (35%)
  Pallas kernels  19.7 us (29%)
  waiting for transfers between devices  18.4 us (27%)
  other arithmetic  3.7 us (5%)
  local copies, waits for them, and re-layouts  1.43 us (2%)
    ppermute x8, starting transfers between devices, along(): return lax.ppermute(block, 'col', pairs)  15.2 us
    pallas_call x6, Pallas kernels, multiply(): pl.pallas_call(functools.partial(multiply_kernel, slots, kinds, rows, wid...  13.4 us
    ppermute x13, waiting for transfers between devices, across(): return lax.ppermute(block, 'row', [(i, i ^ bit) for i in range(8)])  11.7 us
    ppermute x13, starting transfers between devices, across(): return lax.ppermute(block, 'row', [(i, i ^ bit) for i in range(8)])  8.06 us
    ppermute x8, waiting for transfers between devices, along(): return lax.ppermute(block, 'col', pairs)  6.7 us
    pallas_call x7, Pallas kernels, add(): pl.pallas_call(functools.partial(add_kernel, tuple((weight for _, weight...  6.23 us
    select_n x3, other arithmetic, choose(): return jnp.where(core == 0, low, high)  2.03 us
  transfers between devices with their start and end apart: 21, of which 9 were waited for; matrix products, arithmetic and copies ran while one was open for 6% of the time, Pallas kernels for 27%

profile of v1, /device:TPU:10, one launch (start us, length us, event | category | flops | bytes accessed | tf_op | source)
XLA Modules:
  0.0 66.8 jit_solution(2836963345926205293)
XLA Ops:
  0.0 2.1 %collective-permute-done = bf16[2048,128]{1,0:T(8,128)(2,1)S(1)} collective-permute-done((bf16[2048,128]{1,0:T(8,128)(2,1)}, bf16[2048,128]{1,0:T(8,128)(2,1)S(1)}, u32[]{:S(2)}, u32[]{:S(2)}) %collective-permute-start) | collective-permute-done | bytes 524320 | tf_op jit(solution)/shard_map/ppermute | solution.py:205
  2.1 1.0 %slice_select_fusion = bf16[1024,128]{1,0:T(8,128)(2,1)S(1)} fusion(bf16[2048,128]{1,0:T(8,128)(2,1)S(1)} %collective-permute-done, bf16[2048,128]{1,0:T(8,128)(2,1)} %param.5, pred[]{:T(512)S(6)} %eq.4), kind=kLoop, calls=%fused_computation.3 | loop fusion | flops 131072 | bytes 786433 | tf_op jit(solution)/shard_map/jit(_where)/select_n | solution.py:208
  3.1 1.6 %collective-permute-start.3 = (bf16[1024,128]{1,0:T(8,128)(2,1)S(1)}, bf16[1024,128]{1,0:T(8,128)(2,1)S(1)}, u32[]{:S(2)}, u32[]{:S(2)}) collective-permute-start(bf16[1024,128]{1,0:T(8,128)(2,1)S(1)} %slice_select_fusion), channel_id=1, source_target_pairs={{0,24},{4,28},{8,16},{12,20},{16,8},{20,12},{24,0},{28,4},{1,25},{... | collective-permute-start | bytes 786440 | tf_op jit(solution)/shard_map/ppermute | solution.py:205
  4.7 0.5 collective-permute-start.2
  5.2 1.5 %collective-permute-start.1 = (bf16[1024,128]{1,0:T(8,128)(2,1)S(1)}, bf16[1024,128]{1,0:T(8,128)(2,1)S(1)}, u32[]{:S(2)}, u32[]{:S(2)}) collective-permute-start(bf16[1024,128]{1,0:T(8,128)(2,1)S(1)} %slice_select_fusion), channel_id=1, source_target_pairs={{0,8},{4,12},{8,0},{12,4},{16,24},{20,28},{24,16},{28,20},{1,9},{5... | collective-permute-start | bytes 786440 | tf_op jit(solution)/shard_map/ppermute | solution.py:205
  6.7 0.7 %convert_element_type.3 = bf16[8,16]{1,0:T(8,128)(2,1)S(1)} convert(s32[8,16]{1,0:T(8,128)} %param.6) | non-fusion elementwise | flops 128 | bytes 768 | tf_op jit(solution)/shard_map/convert_element_type | solution.py:23
  7.3 1.0 %slice_select_fusion.1 = bf16[1024,128]{1,0:T(8,128)(2,1)S(1)} fusion(bf16[2048,128]{1,0:T(8,128)(2,1)} %param.5, bf16[2048,128]{1,0:T(8,128)(2,1)S(1)} %collective-permute-done, pred[]{:T(512)S(6)} %eq.4), kind=kLoop, calls=%fused_computation.4 | loop fusion | flops 131072 | bytes 786433 | tf_op jit(solution)/shard_map/jit(_where)/select_n | solution.py:208
  8.3 0.6 mul.11
  9.0 0.9 %bitcast_multiply_fusion.a_ref = bf16[1024,2048]{1,0:T(8,128)(2,1)S(1)} fusion(bf16[1024,2048]{1,0:T(8,128)(2,1)S(1)} %copy-done, bf16[128,8,16,128]{3,2,1,0:T(8,128)(2,1)S(1)} %bitcast.8), kind=kLoop, calls=%fused_computation | loop fusion | flops 2097152 | bytes 12582912 | tf_op jit(solution)/shard_map/mul | solution.py:24
  9.9 0.1 copy-done.1
  10.0 0.1 broadcast_select_fusion
  10.1 0.7 %dynamic-slice_bitcast_fusion = s32[7]{0:T(128)S(1)} fusion(s32[4,7]{1,0:T(4,128)} %constant.38.clone, s32[]{:T(128)S(6)} %select_n.41), kind=kLoop, calls=%fused_computation.6 | loop fusion | bytes 60 | tf_op jit(solution)/shard_map/squeeze | solution.py:219
  10.8 0.1 pad_add_fusion.facts
  10.8 2.4 %collective-permute-done.3.refs_3_ = bf16[1024,128]{1,0:T(8,128)(2,1)S(1)} collective-permute-done((bf16[1024,128]{1,0:T(8,128)(2,1)S(1)}, bf16[1024,128]{1,0:T(8,128)(2,1)S(1)}, u32[]{:S(2)}, u32[]{:S(2)}) %collective-permute-start.3) | collective-permute-done | bytes 262176 | tf_op jit(solution)/shard_map/ppermute | solution.py:205
  13.3 4.8 %collective-permute-done.2.refs_2_ = bf16[1024,128]{1,0:T(8,128)(2,1)S(1)} collective-permute-done((bf16[1024,128]{1,0:T(8,128)(2,1)S(1)}, bf16[1024,128]{1,0:T(8,128)(2,1)S(1)}, u32[]{:S(2)}, u32[]{:S(2)}) %collective-permute-start.2) | collective-permute-done | bytes 262176 | tf_op jit(solution)/shard_map/ppermute | solution.py:205
  18.1 0.1 collective-permute-done.1.refs_1_
  18.1 0.4 collective-permute-start.4
  18.5 1.5 %collective-permute-start.10 = (bf16[1024,128]{1,0:T(8,128)(2,1)S(1)}, bf16[1024,128]{1,0:T(8,128)(2,1)S(1)}, u32[]{:S(2)}, u32[]{:S(2)}) collective-permute-start(bf16[1024,128]{1,0:T(8,128)(2,1)S(1)} %slice_select_fusion.1), channel_id=1, source_target_pairs={{0,24},{4,28},{8,16},{12,20},{16,8},{20,12},{24,0},{28,4},{1,25},{... | collective-permute-start | bytes 786440 | tf_op jit(solution)/shard_map/ppermute | solution.py:205
  20.0 0.5 collective-permute-start.9
  20.6 1.5 %collective-permute-start.8 = (bf16[1024,128]{1,0:T(8,128)(2,1)S(1)}, bf16[1024,128]{1,0:T(8,128)(2,1)S(1)}, u32[]{:S(2)}, u32[]{:S(2)}) collective-permute-start(bf16[1024,128]{1,0:T(8,128)(2,1)S(1)} %slice_select_fusion.1), channel_id=1, source_target_pairs={{0,8},{4,12},{8,0},{12,4},{16,24},{20,28},{24,16},{28,20},{1,9},{5... | collective-permute-start | bytes 786440 | tf_op jit(solution)/shard_map/ppermute | solution.py:205
  22.0 2.2 %shard_map.46 = s16[1040,128]{1,0:T(8,128)(2,1)S(1)} custom-call(s32[9]{0:T(128)S(1)} %pad_add_fusion.facts, bf16[1024,2048]{1,0:T(8,128)(2,1)S(1)} %bitcast_multiply_fusion.a_ref, bf16[2048,128]{1,0:T(8,128)(2,1)S(1)} %get-tuple-element.66.refs_0_, bf16[1024,128]{1,0:T(8,128)(2,1)S(1)} %collective-permute-done.1.refs_1_, ...), custom_call_target="tpu_custom_call" | custom-call | flops 3000000000 | bytes 9000000 | tf_op jit(solution)/shard_map/pallas_call | solution.py:122
  24.3 0.5 collective-permute-start.7
  24.8 2.2 %shard_map.47 = (s16[1040,128]{1,0:T(8,128)(2,1)S(1)}, f32[1024,128]{1,0:T(8,128)S(1)}) custom-call(s32[9]{0:T(128)S(1)} %pad_add_fusion.facts, bf16[1024,2048]{1,0:T(8,128)(2,1)S(1)} %bitcast_multiply_fusion.a_ref, bf16[2048,128]{1,0:T(8,128)(2,1)S(1)} %get-tuple-element.66.refs_0_, bf16[1024,128]{1,0:T(8,128)(2,1)S(1)} %collective-permute-done.1.refs_1_, ...), custom_call_target="tpu_custom_call" | custom-call | flops 3000000000 | bytes 9000000 | tf_op jit(solution)/shard_map/pallas_call | solution.py:122
  27.0 1.7 %collective-permute-start.14 = (s16[1040,128]{1,0:T(8,128)(2,1)S(1)}, s16[1040,128]{1,0:T(8,128)(2,1)S(1)}, u32[]{:S(2)}, u32[]{:S(2)}) collective-permute-start(s16[1040,128]{1,0:T(8,128)(2,1)S(1)} %get-tuple-element.45), channel_id=1, source_target_pairs={{0,1},{1,0},{2,3},{3,2},{4,5},{5,4},{6,7},{7,6},{8,9},{9,8},{10,11... | collective-permute-start | bytes 798728 | tf_op jit(solution)/shard_map/ppermute | solution.py:211
  28.7 2.3 %shard_map.48 = (f32[1024,128]{1,0:T(8,128)S(1)}, f32[1024,128]{1,0:T(8,128)S(1)}) custom-call(s32[9]{0:T(128)S(1)} %pad_add_fusion.facts, bf16[1024,2048]{1,0:T(8,128)(2,1)S(1)} %bitcast_multiply_fusion.a_ref, bf16[2048,128]{1,0:T(8,128)(2,1)S(1)} %get-tuple-element.66.refs_0_, bf16[1024,128]{1,0:T(8,128)(2,1)S(1)} %collective-permute-done.1.refs_1_, ...), custom_call_target="tpu_custom_call" | custom-call | flops 3000000000 | bytes 9000000 | tf_op jit(solution)/shard_map/pallas_call | solution.py:122
  31.0 0.1 collective-permute-start.13
  31.1 2.3 %collective-permute-done.9.refs_2_ = bf16[1024,128]{1,0:T(8,128)(2,1)S(1)} collective-permute-done((bf16[1024,128]{1,0:T(8,128)(2,1)S(1)}, bf16[1024,128]{1,0:T(8,128)(2,1)S(1)}, u32[]{:S(2)}, u32[]{:S(2)}) %collective-permute-start.9) | collective-permute-done | bytes 262176 | tf_op jit(solution)/shard_map/ppermute | solution.py:205
  33.4 0.5 collective-permute-start.11
  33.9 0.8 %shard_map.49 = s16[1040,128]{1,0:T(8,128)(2,1)S(1)} custom-call(s32[9]{0:T(128)S(1)} %pad_add_fusion.facts, f32[1024,128]{1,0:T(8,128)S(1)} %get-tuple-element.47.refs_0_, s16[1040,128]{1,0:T(8,128)(2,1)S(1)} %collective-permute-done.7.refs_1_), custom_call_target="tpu_custom_call" | custom-call | flops 3000000000 | bytes 9000000 | tf_op jit(solution)/shard_map/pallas_call | solution.py:172
  34.7 2.6 %collective-permute-start.15 = (s16[1040,128]{1,0:T(8,128)(2,1)S(1)}, s16[1040,128]{1,0:T(8,128)(2,1)S(1)}, u32[]{:S(2)}, u32[]{:S(2)}) collective-permute-start(s16[1040,128]{1,0:T(8,128)(2,1)S(1)} %shard_map.49), channel_id=1, source_target_pairs={{0,1},{1,3},{2,0},{3,2},{4,5},{5,7},{6,4},{7,6},{8,9},{9,11},{10,8... | collective-permute-start | bytes 798728 | tf_op jit(solution)/shard_map/ppermute | solution.py:211
  37.4 2.2 %shard_map.50 = s16[1040,128]{1,0:T(8,128)(2,1)S(1)} custom-call(s32[9]{0:T(128)S(1)} %pad_add_fusion.facts, bf16[1024,2048]{1,0:T(8,128)(2,1)S(1)} %bitcast_multiply_fusion.a_ref, bf16[2048,128]{1,0:T(8,128)(2,1)S(1)} %get-tuple-element.65.refs_0_, bf16[1024,128]{1,0:T(8,128)(2,1)S(1)} %collective-permute-done.8.refs_1_, ...), custom_call_target="tpu_custom_call" | custom-call | flops 3000000000 | bytes 9000000 | tf_op jit(solution)/shard_map/pallas_call | solution.py:122
  39.6 0.1 collective-permute-start.16
  39.6 2.2 %shard_map.51 = (s16[1040,128]{1,0:T(8,128)(2,1)S(1)}, f32[1024,128]{1,0:T(8,128)S(1)}) custom-call(s32[9]{0:T(128)S(1)} %pad_add_fusion.facts, bf16[1024,2048]{1,0:T(8,128)(2,1)S(1)} %bitcast_multiply_fusion.a_ref, bf16[2048,128]{1,0:T(8,128)(2,1)S(1)} %get-tuple-element.65.refs_0_, bf16[1024,128]{1,0:T(8,128)(2,1)S(1)} %collective-permute-done.8.refs_1_, ...), custom_call_target="tpu_custom_call" | custom-call | flops 3000000000 | bytes 9000000 | tf_op jit(solution)/shard_map/pallas_call | solution.py:122
  41.9 1.3 %collective-permute-start.18 = (s16[1040,128]{1,0:T(8,128)(2,1)S(1)}, s16[1040,128]{1,0:T(8,128)(2,1)S(1)}, u32[]{:S(2)}, u32[]{:S(2)}) collective-permute-start(s16[1040,128]{1,0:T(8,128)(2,1)S(1)} %get-tuple-element.54), channel_id=1, source_target_pairs={{0,1},{3,2},{4,5},{7,6},{8,9},{11,10},{12,13},{15,14},{16,17},{19,... | collective-permute-start | bytes 798728 | tf_op jit(solution)/shard_map/ppermute | solution.py:211
  43.2 0.8 %shard_map.52 = s16[1040,128]{1,0:T(8,128)(2,1)S(1)} custom-call(s32[9]{0:T(128)S(1)} %pad_add_fusion.facts, f32[1024,128]{1,0:T(8,128)S(1)} %get-tuple-element.56.refs_0_, s16[1040,128]{1,0:T(8,128)(2,1)S(1)} %collective-permute-done.14.refs_1_), custom_call_target="tpu_custom_call" | custom-call | flops 3000000000 | bytes 9000000 | tf_op jit(solution)/shard_map/pallas_call | solution.py:172
  44.0 3.0 %collective-permute-start.17 = (s16[1040,128]{1,0:T(8,128)(2,1)S(1)}, s16[1040,128]{1,0:T(8,128)(2,1)S(1)}, u32[]{:S(2)}, u32[]{:S(2)}) collective-permute-start(s16[1040,128]{1,0:T(8,128)(2,1)S(1)} %shard_map.52), channel_id=1, source_target_pairs={{1,2},{2,1},{5,6},{6,5},{9,10},{10,9},{13,14},{14,13},{17,18},{18,... | collective-permute-start | bytes 798728 | tf_op jit(solution)/shard_map/ppermute | solution.py:211
  47.0 2.3 %shard_map.53 = (f32[1024,128]{1,0:T(8,128)S(1)}, f32[1024,128]{1,0:T(8,128)S(1)}) custom-call(s32[9]{0:T(128)S(1)} %pad_add_fusion.facts, bf16[1024,2048]{1,0:T(8,128)(2,1)S(1)} %bitcast_multiply_fusion.a_ref, bf16[2048,128]{1,0:T(8,128)(2,1)S(1)} %get-tuple-element.65.refs_0_, bf16[1024,128]{1,0:T(8,128)(2,1)S(1)} %collective-permute-done.8.refs_1_, ...), custom_call_target="tpu_custom_call" | custom-call | flops 3000000000 | bytes 9000000 | tf_op jit(solution)/shard_map/pallas_call | solution.py:122
  49.3 0.4 collective-permute-done.16.refs_1_
  49.7 0.8 %shard_map.54 = s16[1040,128]{1,0:T(8,128)(2,1)S(1)} custom-call(s32[9]{0:T(128)S(1)} %pad_add_fusion.facts, f32[1024,128]{1,0:T(8,128)S(1)} %get-tuple-element.58.refs_0_, s16[1040,128]{1,0:T(8,128)(2,1)S(1)} %collective-permute-done.16.refs_1_), custom_call_target="tpu_custom_call" | custom-call | flops 3000000000 | bytes 9000000 | tf_op jit(solution)/shard_map/pallas_call | solution.py:172
  50.5 2.6 %collective-permute-start.19 = (s16[1040,128]{1,0:T(8,128)(2,1)S(1)}, s16[1040,128]{1,0:T(8,128)(2,1)S(1)}, u32[]{:S(2)}, u32[]{:S(2)}) collective-permute-start(s16[1040,128]{1,0:T(8,128)(2,1)S(1)} %shard_map.54), channel_id=1, source_target_pairs={{0,1},{1,3},{2,0},{3,2},{4,5},{5,7},{6,4},{7,6},{8,9},{9,11},{10,8... | collective-permute-start | bytes 798728 | tf_op jit(solution)/shard_map/ppermute | solution.py:211
  53.1 1.6 %collective-permute-done.17.refs_3_ = s16[1040,128]{1,0:T(8,128)(2,1)S(1)} collective-permute-done((s16[1040,128]{1,0:T(8,128)(2,1)S(1)}, s16[1040,128]{1,0:T(8,128)(2,1)S(1)}, u32[]{:S(2)}, u32[]{:S(2)}) %collective-permute-start.17) | collective-permute-done | bytes 266272 | tf_op jit(solution)/shard_map/ppermute | solution.py:211
  54.8 0.7 collective-permute-done.18.refs_1_
  55.4 0.8 %shard_map.55 = s16[1040,128]{1,0:T(8,128)(2,1)S(1)} custom-call(s32[9]{0:T(128)S(1)} %pad_add_fusion.facts, f32[1024,128]{1,0:T(8,128)S(1)} %get-tuple-element.60.refs_0_, s16[1040,128]{1,0:T(8,128)(2,1)S(1)} %collective-permute-done.18.refs_1_), custom_call_target="tpu_custom_call" | custom-call | flops 3000000000 | bytes 9000000 | tf_op jit(solution)/shard_map/pallas_call | solution.py:172
  56.2 3.5 %collective-permute-start.20 = (s16[1040,128]{1,0:T(8,128)(2,1)S(1)}, s16[1040,128]{1,0:T(8,128)(2,1)S(1)}, u32[]{:S(2)}, u32[]{:S(2)}) collective-permute-start(s16[1040,128]{1,0:T(8,128)(2,1)S(1)} %shard_map.55), channel_id=1, source_target_pairs={{1,2},{2,1},{5,6},{6,5},{9,10},{10,9},{13,14},{14,13},{17,18},{18,... | collective-permute-start | bytes 798728 | tf_op jit(solution)/shard_map/ppermute | solution.py:211
  59.7 0.9 %shard_map.56.refs_2_ = bf16[1024,128]{1,0:T(8,128)(2,1)S(1)} custom-call(s32[9]{0:T(128)S(1)} %pad_add_fusion.facts, f32[1024,128]{1,0:T(8,128)S(1)} %get-tuple-element.62.refs_0_, s16[1040,128]{1,0:T(8,128)(2,1)S(1)} %collective-permute-done.7.refs_1_, s16[1040,128]{1,0:T(8,128)(2,1)S(1)} %collective-permute-done.15.refs_2_, ...), custom_call_target="tpu_custom_call" | custom-call | flops 3000000000 | bytes 9000000 | tf_op jit(solution)/shard_map/pallas_call | solution.py:172
  60.6 0.8 %shard_map.57.refs_0_ = f32[1024,128]{1,0:T(8,128)S(1)} custom-call(s32[9]{0:T(128)S(1)} %pad_add_fusion.facts, f32[1024,128]{1,0:T(8,128)S(1)} %get-tuple-element.64.refs_0_, s16[1040,128]{1,0:T(8,128)(2,1)S(1)} %collective-permute-done.16.refs_1_, s16[1040,128]{1,0:T(8,128)(2,1)S(1)} %collective-permute-done.19.refs_2_), custom_call_target="tpu_custom_call" | custom-call | flops 3000000000 | bytes 9000000 | tf_op jit(solution)/shard_map/pallas_call | solution.py:172
  61.4 4.0 %collective-permute-done.20.refs_1_ = s16[1040,128]{1,0:T(8,128)(2,1)S(1)} collective-permute-done((s16[1040,128]{1,0:T(8,128)(2,1)S(1)}, s16[1040,128]{1,0:T(8,128)(2,1)S(1)}, u32[]{:S(2)}, u32[]{:S(2)}) %collective-permute-start.20) | collective-permute-done | bytes 266272 | tf_op jit(solution)/shard_map/ppermute | solution.py:211
  65.3 1.4 %shard_map.58 = bf16[1024,256]{1,0:T(8,128)(2,1)} custom-call(s32[9]{0:T(128)S(1)} %pad_add_fusion.facts, f32[1024,128]{1,0:T(8,128)S(1)} %shard_map.57.refs_0_, s16[1040,128]{1,0:T(8,128)(2,1)S(1)} %collective-permute-done.20.refs_1_, bf16[1024,128]{1,0:T(8,128)(2,1)S(1)} %shard_map.56.refs_2_), custom_call_target="tpu_custom_call" | custom-call | flops 3000000000 | bytes 9000000 | tf_op jit(solution)/shard_map/pallas_call | solution.py:172
  (19 shorter events, 0.1 us)
Async XLA Ops:
  0.0 2.1 %collective-permute-start = (bf16[2048,128]{1,0:T(8,128)(2,1)}, bf16[2048,128]{1,0:T(8,128)(2,1)S(1)}, u32[]{:S(2)}, u32[]{:S(2)}) collective-permute-start(bf16[2048,128]{1,0:T(8,128)(2,1)} %param.5), channel_id=1, source_target_pairs={{0,4},{4,0},{8,12},{12,8},{16,20},{20,16},{24,28},{28,24},{1,5},{5... | collective-permute-start | bytes 1572872 | tf_op jit(solution)/shard_map/ppermute | solution.py:205
  0.0 8.9 %copy-start = (bf16[1024,2048]{1,0:T(8,128)(2,1)S(1)}, bf16[1024,2048]{1,0:T(8,128)(2,1)}, u32[]{:S(2)}) copy-start(bf16[1024,2048]{1,0:T(8,128)(2,1)} %param.4) | copy-start | bytes 12582916
  3.1 10.2 %collective-permute-start.3 = (bf16[1024,128]{1,0:T(8,128)(2,1)S(1)}, bf16[1024,128]{1,0:T(8,128)(2,1)S(1)}, u32[]{:S(2)}, u32[]{:S(2)}) collective-permute-start(bf16[1024,128]{1,0:T(8,128)(2,1)S(1)} %slice_select_fusion), channel_id=1, source_target_pairs={{0,24},{4,28},{8,16},{12,20},{16,8},{20,12},{24,0},{28,4},{1,25},{... | collective-permute-start | bytes 786440 | tf_op jit(solution)/shard_map/ppermute | solution.py:205
  4.7 13.4 %collective-permute-start.2 = (bf16[1024,128]{1,0:T(8,128)(2,1)S(1)}, bf16[1024,128]{1,0:T(8,128)(2,1)S(1)}, u32[]{:S(2)}, u32[]{:S(2)}) collective-permute-start(bf16[1024,128]{1,0:T(8,128)(2,1)S(1)} %slice_select_fusion), channel_id=1, source_target_pairs={{0,16},{4,20},{8,24},{12,28},{16,0},{20,4},{24,8},{28,12},{1,17},{... | collective-permute-start | bytes 786440 | tf_op jit(solution)/shard_map/ppermute | solution.py:205
  5.2 13.0 %collective-permute-start.1 = (bf16[1024,128]{1,0:T(8,128)(2,1)S(1)}, bf16[1024,128]{1,0:T(8,128)(2,1)S(1)}, u32[]{:S(2)}, u32[]{:S(2)}) collective-permute-start(bf16[1024,128]{1,0:T(8,128)(2,1)S(1)} %slice_select_fusion), channel_id=1, source_target_pairs={{0,8},{4,12},{8,0},{12,4},{16,24},{20,28},{24,16},{28,20},{1,9},{5... | collective-permute-start | bytes 786440 | tf_op jit(solution)/shard_map/ppermute | solution.py:205
  9.0 1.0 %copy-start.1 = (bf16[2048,128]{1,0:T(8,128)(2,1)S(1)}, bf16[2048,128]{1,0:T(8,128)(2,1)}, u32[]{:S(2)}) copy-start(bf16[2048,128]{1,0:T(8,128)(2,1)} %param.5) | copy-start | bytes 1572868
  13.3 7.3 %collective-permute-start.6 = (bf16[1024,128]{1,0:T(8,128)(2,1)S(1)}, bf16[1024,128]{1,0:T(8,128)(2,1)S(1)}, u32[]{:S(2)}, u32[]{:S(2)}) collective-permute-start(bf16[1024,128]{1,0:T(8,128)(2,1)S(1)} %collective-permute-done.3.refs_3_), channel_id=1, source_target_pairs={{0,4},{4,0},{8,12},{12,8},{16,20},{20,16},{24,28},{28,24},{1,5},{5... | collective-permute-start | bytes 786440 | tf_op jit(solution)/shard_map/ppermute | solution.py:205
  18.0 4.0 %collective-permute-start.5 = (bf16[1024,128]{1,0:T(8,128)(2,1)S(1)}, bf16[1024,128]{1,0:T(8,128)(2,1)S(1)}, u32[]{:S(2)}, u32[]{:S(2)}) collective-permute-start(bf16[1024,128]{1,0:T(8,128)(2,1)S(1)} %collective-permute-done.2.refs_2_), channel_id=1, source_target_pairs={{0,4},{4,0},{8,12},{12,8},{16,20},{20,16},{24,28},{28,24},{1,5},{5... | collective-permute-start | bytes 786440 | tf_op jit(solution)/shard_map/ppermute | solution.py:205
  18.1 3.9 %collective-permute-start.4 = (bf16[1024,128]{1,0:T(8,128)(2,1)S(1)}, bf16[1024,128]{1,0:T(8,128)(2,1)S(1)}, u32[]{:S(2)}, u32[]{:S(2)}) collective-permute-start(bf16[1024,128]{1,0:T(8,128)(2,1)S(1)} %collective-permute-done.1.refs_1_), channel_id=1, source_target_pairs={{0,4},{4,0},{8,12},{12,8},{16,20},{20,16},{24,28},{28,24},{1,5},{5... | collective-permute-start | bytes 786440 | tf_op jit(solution)/shard_map/ppermute | solution.py:205
  18.5 12.4 %collective-permute-start.10 = (bf16[1024,128]{1,0:T(8,128)(2,1)S(1)}, bf16[1024,128]{1,0:T(8,128)(2,1)S(1)}, u32[]{:S(2)}, u32[]{:S(2)}) collective-permute-start(bf16[1024,128]{1,0:T(8,128)(2,1)S(1)} %slice_select_fusion.1), channel_id=1, source_target_pairs={{0,24},{4,28},{8,16},{12,20},{16,8},{20,12},{24,0},{28,4},{1,25},{... | collective-permute-start | bytes 786440 | tf_op jit(solution)/shard_map/ppermute | solution.py:205
  20.0 13.3 %collective-permute-start.9 = (bf16[1024,128]{1,0:T(8,128)(2,1)S(1)}, bf16[1024,128]{1,0:T(8,128)(2,1)S(1)}, u32[]{:S(2)}, u32[]{:S(2)}) collective-permute-start(bf16[1024,128]{1,0:T(8,128)(2,1)S(1)} %slice_select_fusion.1), channel_id=1, source_target_pairs={{0,16},{4,20},{8,24},{12,28},{16,0},{20,4},{24,8},{28,12},{1,17},{... | collective-permute-start | bytes 786440 | tf_op jit(solution)/shard_map/ppermute | solution.py:205
  20.6 12.8 %collective-permute-start.8 = (bf16[1024,128]{1,0:T(8,128)(2,1)S(1)}, bf16[1024,128]{1,0:T(8,128)(2,1)S(1)}, u32[]{:S(2)}, u32[]{:S(2)}) collective-permute-start(bf16[1024,128]{1,0:T(8,128)(2,1)S(1)} %slice_select_fusion.1), channel_id=1, source_target_pairs={{0,8},{4,12},{8,0},{12,4},{16,24},{20,28},{24,16},{28,20},{1,9},{5... | collective-permute-start | bytes 786440 | tf_op jit(solution)/shard_map/ppermute | solution.py:205
  24.3 9.6 %collective-permute-start.7 = (s16[1040,128]{1,0:T(8,128)(2,1)S(1)}, s16[1040,128]{1,0:T(8,128)(2,1)S(1)}, u32[]{:S(2)}, u32[]{:S(2)}) collective-permute-start(s16[1040,128]{1,0:T(8,128)(2,1)S(1)} %shard_map.46), channel_id=1, source_target_pairs={{0,1},{1,0},{2,3},{3,2},{4,5},{5,4},{6,7},{7,6},{8,9},{9,8},{10,11... | collective-permute-start | bytes 798728 | tf_op jit(solution)/shard_map/ppermute | solution.py:211
  27.0 16.2 %collective-permute-start.14 = (s16[1040,128]{1,0:T(8,128)(2,1)S(1)}, s16[1040,128]{1,0:T(8,128)(2,1)S(1)}, u32[]{:S(2)}, u32[]{:S(2)}) collective-permute-start(s16[1040,128]{1,0:T(8,128)(2,1)S(1)} %get-tuple-element.45), channel_id=1, source_target_pairs={{0,1},{1,0},{2,3},{3,2},{4,5},{5,4},{6,7},{7,6},{8,9},{9,8},{10,11... | collective-permute-start | bytes 798728 | tf_op jit(solution)/shard_map/ppermute | solution.py:211
  31.0 6.4 %collective-permute-start.13 = (bf16[1024,128]{1,0:T(8,128)(2,1)S(1)}, bf16[1024,128]{1,0:T(8,128)(2,1)S(1)}, u32[]{:S(2)}, u32[]{:S(2)}) collective-permute-start(bf16[1024,128]{1,0:T(8,128)(2,1)S(1)} %collective-permute-done.10.refs_3_), channel_id=1, source_target_pairs={{0,4},{4,0},{8,12},{12,8},{16,20},{20,16},{24,28},{28,24},{1,5},{5... | collective-permute-start | bytes 786440 | tf_op jit(solution)/shard_map/ppermute | solution.py:205
  33.4 4.0 %collective-permute-start.12 = (bf16[1024,128]{1,0:T(8,128)(2,1)S(1)}, bf16[1024,128]{1,0:T(8,128)(2,1)S(1)}, u32[]{:S(2)}, u32[]{:S(2)}) collective-permute-start(bf16[1024,128]{1,0:T(8,128)(2,1)S(1)} %collective-permute-done.9.refs_2_), channel_id=1, source_target_pairs={{0,4},{4,0},{8,12},{12,8},{16,20},{20,16},{24,28},{28,24},{1,5},{5... | collective-permute-start | bytes 786440 | tf_op jit(solution)/shard_map/ppermute | solution.py:205
  33.4 4.0 %collective-permute-start.11 = (bf16[1024,128]{1,0:T(8,128)(2,1)S(1)}, bf16[1024,128]{1,0:T(8,128)(2,1)S(1)}, u32[]{:S(2)}, u32[]{:S(2)}) collective-permute-start(bf16[1024,128]{1,0:T(8,128)(2,1)S(1)} %collective-permute-done.8.refs_1_), channel_id=1, source_target_pairs={{0,4},{4,0},{8,12},{12,8},{16,20},{20,16},{24,28},{28,24},{1,5},{5... | collective-permute-start | bytes 786440 | tf_op jit(solution)/shard_map/ppermute | solution.py:205
  34.7 12.3 %collective-permute-start.15 = (s16[1040,128]{1,0:T(8,128)(2,1)S(1)}, s16[1040,128]{1,0:T(8,128)(2,1)S(1)}, u32[]{:S(2)}, u32[]{:S(2)}) collective-permute-start(s16[1040,128]{1,0:T(8,128)(2,1)S(1)} %shard_map.49), channel_id=1, source_target_pairs={{0,1},{1,3},{2,0},{3,2},{4,5},{5,7},{6,4},{7,6},{8,9},{9,11},{10,8... | collective-permute-start | bytes 798728 | tf_op jit(solution)/shard_map/ppermute | solution.py:211
  39.6 10.2 %collective-permute-start.16 = (s16[1040,128]{1,0:T(8,128)(2,1)S(1)}, s16[1040,128]{1,0:T(8,128)(2,1)S(1)}, u32[]{:S(2)}, u32[]{:S(2)}) collective-permute-start(s16[1040,128]{1,0:T(8,128)(2,1)S(1)} %shard_map.50), channel_id=1, source_target_pairs={{0,1},{1,0},{2,3},{3,2},{4,5},{5,4},{6,7},{7,6},{8,9},{9,8},{10,11... | collective-permute-start | bytes 798728 | tf_op jit(solution)/shard_map/ppermute | solution.py:211
  41.9 13.5 %collective-permute-start.18 = (s16[1040,128]{1,0:T(8,128)(2,1)S(1)}, s16[1040,128]{1,0:T(8,128)(2,1)S(1)}, u32[]{:S(2)}, u32[]{:S(2)}) collective-permute-start(s16[1040,128]{1,0:T(8,128)(2,1)S(1)} %get-tuple-element.54), channel_id=1, source_target_pairs={{0,1},{3,2},{4,5},{7,6},{8,9},{11,10},{12,13},{15,14},{16,17},{19,... | collective-permute-start | bytes 798728 | tf_op jit(solution)/shard_map/ppermute | solution.py:211
  44.0 10.8 %collective-permute-start.17 = (s16[1040,128]{1,0:T(8,128)(2,1)S(1)}, s16[1040,128]{1,0:T(8,128)(2,1)S(1)}, u32[]{:S(2)}, u32[]{:S(2)}) collective-permute-start(s16[1040,128]{1,0:T(8,128)(2,1)S(1)} %shard_map.52), channel_id=1, source_target_pairs={{1,2},{2,1},{5,6},{6,5},{9,10},{10,9},{13,14},{14,13},{17,18},{18,... | collective-permute-start | bytes 798728 | tf_op jit(solution)/shard_map/ppermute | solution.py:211
  50.5 10.1 %collective-permute-start.19 = (s16[1040,128]{1,0:T(8,128)(2,1)S(1)}, s16[1040,128]{1,0:T(8,128)(2,1)S(1)}, u32[]{:S(2)}, u32[]{:S(2)}) collective-permute-start(s16[1040,128]{1,0:T(8,128)(2,1)S(1)} %shard_map.54), channel_id=1, source_target_pairs={{0,1},{1,3},{2,0},{3,2},{4,5},{5,7},{6,4},{7,6},{8,9},{9,11},{10,8... | collective-permute-start | bytes 798728 | tf_op jit(solution)/shard_map/ppermute | solution.py:211
  56.2 9.1 %collective-permute-start.20 = (s16[1040,128]{1,0:T(8,128)(2,1)S(1)}, s16[1040,128]{1,0:T(8,128)(2,1)S(1)}, u32[]{:S(2)}, u32[]{:S(2)}) collective-permute-start(s16[1040,128]{1,0:T(8,128)(2,1)S(1)} %shard_map.55), channel_id=1, source_target_pairs={{1,2},{2,1},{5,6},{6,5},{9,10},{10,9},{13,14},{14,13},{17,18},{18,... | collective-permute-start | bytes 798728 | tf_op jit(solution)/shard_map/ppermute | solution.py:211

commit v2 on v1

v2 whole, which is shorter than its diff:
```python
import functools

import jax
import jax.numpy as jnp
from jax import lax
from jax.experimental import pallas as pl
from jax.experimental.pallas import tpu as pltpu
from jax.sharding import PartitionSpec as P

TILE = 128
CODE_ROWS = 16
LEVELS = 32767.0
STEPS_PER_OCTAVE = 64.0
BLOCK_ROWS = 512
ADD_ROWS = 512


def apply_mask(amplitudes, tile_mask):
    tiles_m, tiles_k = tile_mask.shape
    tile_rows = amplitudes.shape[0] // tiles_m
    tile_cols = amplitudes.shape[1] // tiles_k
    blocks = amplitudes.reshape(tiles_m, tile_rows, tiles_k, tile_cols)
    weights = tile_mask.astype(amplitudes.dtype)[:, None, :, None]
    return (blocks * weights).reshape(amplitudes.shape)


def general(amplitudes, integrals, tile_mask):
    masked = apply_mask(amplitudes, tile_mask)
    partial_sums = jnp.dot(
        masked,
        lax.all_gather(integrals, "row", axis=1, tiled=True),
        preferred_element_type=jnp.float32,
    )
    summed = lax.psum_scatter(partial_sums, "col", scatter_dimension=1, tiled=True)
    return summed.astype(jnp.bfloat16)


def decode(ref, step, rows, block_rows, weight):
    groups = block_rows // TILE
    start = pl.multiple_of(step * block_rows, block_rows)
    levels = ref[pl.ds(start, block_rows), :].astype(jnp.int32).astype(jnp.float32)
    codes = ref[pl.ds(rows, CODE_ROWS), :].astype(jnp.int32).astype(jnp.float32)
    pieces = []
    which = lax.broadcasted_iota(jnp.int32, codes.shape, 0)
    for g in range(groups):
        code = jnp.sum(jnp.where(which == step * groups + g, codes, 0.0), axis=0, keepdims=True)
        unit = jnp.exp2(code / STEPS_PER_OCTAVE) * (weight / LEVELS)
        pieces.append(levels[g * TILE : (g + 1) * TILE] * unit)
    return jnp.concatenate(pieces, axis=0)


def encode(acc, step, out_ref, code_ref, rows):
    block_rows = acc.shape[0]
    groups = block_rows // TILE
    pieces = []
    for g in range(groups):
        part = acc[g * TILE : (g + 1) * TILE]
        largest = jnp.max(jnp.abs(part), axis=0, keepdims=True)
        code = jnp.ceil(jnp.log(jnp.maximum(largest, 1e-30)) * (STEPS_PER_OCTAVE / 0.6931471805599453))
        scaled = jnp.round(part * (jnp.exp2(-code / STEPS_PER_OCTAVE) * LEVELS))
        pieces.append(jnp.clip(scaled, -LEVELS, LEVELS).astype(jnp.int32))
        code_ref[pl.ds(step * groups + g, 1), :] = code
    start = pl.multiple_of(step * block_rows, block_rows)
    out_ref[pl.ds(start, block_rows), :] = jnp.concatenate(pieces, axis=0).astype(jnp.int16)

    @pl.when(step == pl.num_programs(0) - 1)
    def _():
        out_ref[pl.ds(rows, CODE_ROWS), :] = code_ref[...].astype(jnp.int32).astype(jnp.int16)


def fetch(chosen, core, mine, other, b, first, sem):
    width = mine[0].shape[1]
    here = pl.ds(pl.multiple_of(first + core * width, width), width)
    there = pl.ds(pl.multiple_of(first + (1 - core) * width, width), width)
    for j in range(len(mine)):

        @pl.when(chosen == j)
        def _():
            pltpu.make_async_copy(mine[j], b.at[:, here], sem).start()
            pltpu.make_async_copy(other[j], b.at[:, there], sem).start()


def multiply_kernel(slots, kinds, rows, width, sources, facts, a_ref, *refs):
    mine, other, refs = refs[:sources], refs[sources : 2 * sources], refs[2 * sources :]
    count = sum(len(kind) for kind in kinds)
    outs, refs = list(refs[:count]), refs[count:]
    b, sems, codes = refs[0], refs[1], list(refs[2:])
    step = pl.program_id(0)

    @pl.when(step == 0)
    def _():
        for j, slot in enumerate(slots):
            fetch(facts[slot] ^ facts[CHIP], facts[CORE], mine, other, b, j * width, sems.at[j])
        for j in range(len(slots)):
            span = b.at[:, pl.ds(j * width, width)]
            pltpu.make_async_copy(span, span, sems.at[j]).wait()

    acc = jnp.dot(a_ref[...], b[...], preferred_element_type=jnp.float32)
    for j, kind in enumerate(kinds):
        part = acc[:, j * width : (j + 1) * width]
        for form in kind:
            out_ref = outs.pop(0)
            if form == "coded":
                encode(part, step, out_ref, codes.pop(0), rows)
            else:
                out_ref[...] = part


def multiply(facts, masked, columns, slots, kinds):
    rows, depth = masked.shape
    sources = len(columns) // 2
    width = columns[0].shape[1] * 2
    packed = (rows + CODE_ROWS, width)
    forms = [form for kind in kinds for form in kind]
    coded = (pl.BlockSpec(packed, lambda i, c: (0, 0)), jax.ShapeDtypeStruct(packed, jnp.int16))
    plain = (pl.BlockSpec((BLOCK_ROWS, width), lambda i, c: (i, 0)), jax.ShapeDtypeStruct((rows, width), jnp.float32))
    outs = [coded if form == "coded" else plain for form in forms]
    return pl.pallas_call(
        functools.partial(multiply_kernel, slots, kinds, rows, width, sources),
        out_shape=[shape for _, shape in outs],
        grid_spec=pltpu.PrefetchScalarGridSpec(
            num_scalar_prefetch=1,
            grid=(rows // BLOCK_ROWS,),
            in_specs=[pl.BlockSpec((BLOCK_ROWS, depth), lambda i, c: (i, 0))]
            + [pl.BlockSpec(memory_space=pl.ANY)] * len(columns),
            out_specs=[spec for spec, _ in outs],
            scratch_shapes=[pltpu.VMEM((depth, width * len(slots)), masked.dtype), pltpu.SemaphoreType.DMA((len(slots),))]
            + [pltpu.VMEM((CODE_ROWS, width), jnp.float32)] * forms.count("coded"),
        ),
        compiler_params=pltpu.CompilerParams(vmem_limit_bytes=24 * 1024 * 1024),
        cost_estimate=pl.CostEstimate(flops=3000000000, bytes_accessed=9000000, transcendentals=0),
    )(facts, masked, *columns)


def add_kernel(terms, rows, facts, *refs):
    step = pl.program_id(0)
    blocks, refs = refs[: len(terms)], refs[len(terms) :]
    acc = None
    for block, weight in zip(blocks, terms):
        share = facts[weight].astype(jnp.float32)
        if block.dtype == jnp.int16:
            value = decode(block, step, rows, ADD_ROWS, share)
        else:
            value = block[...] if weight == ALWAYS else block[...] * share
        acc = value if acc is None else acc + value
    if refs[0].dtype == jnp.int16:
        encode(acc, step, refs[0], refs[1], rows)
    else:
        refs[0][...] = acc.astype(refs[0].dtype)


def add(facts, terms, dtype=jnp.int16):
    rows, width = next(x.shape for x, _ in terms if x.dtype == jnp.float32)
    packed = (rows + CODE_ROWS, width)
    plain = pl.BlockSpec((ADD_ROWS, width), lambda i, c: (i, 0))
    coded = pl.BlockSpec(packed, lambda i, c: (0, 0))
    if dtype == jnp.int16:
        out_spec, out_shape = coded, jax.ShapeDtypeStruct(packed, dtype)
        scratch = [pltpu.VMEM((CODE_ROWS, width), jnp.float32)]
    else:
        out_spec, out_shape = plain, jax.ShapeDtypeStruct((rows, width), dtype)
        scratch = []
    return pl.pallas_call(
        functools.partial(add_kernel, tuple(weight for _, weight in terms), rows),
        out_shape=out_shape,
        grid_spec=pltpu.PrefetchScalarGridSpec(
            num_scalar_prefetch=1,
            grid=(rows // ADD_ROWS,),
            in_specs=[coded if x.dtype == jnp.int16 else plain for x, _ in terms],
            out_specs=out_spec,
            scratch_shapes=scratch,
        ),
        compiler_params=pltpu.CompilerParams(vmem_limit_bytes=16 * 1024 * 1024),
        cost_estimate=pl.CostEstimate(flops=3000000000, bytes_accessed=9000000, transcendentals=0),
    )(facts, *[x for x, _ in terms])


def plan_of(chip, at):
    end = at in (0, 3)
    far, near = (3, 2) if at < 2 else (0, 1)
    late = chip == (0 if at < 2 else 3)
    passed = (near, far) if late else (far, near)
    home = 0 if at < 2 else 3
    if end:
        first, second, third, relayed = passed[0], passed[1], 3 - near, (chip, chip)
    else:
        straight = chip ^ home != 3
        first, second = (home, chip) if straight else (chip, home)
        third, relayed = chip, passed
    return (first, second, third, *relayed, at, 1, int(end), int(not end))


FIRST, SECOND, THIRD, RELAY_ONE, RELAY_TWO, HERE, ALWAYS, OUTER, INNER, CORE, CHIP = range(11)


def line_pairs(choose):
    return [(row * 4 + a, row * 4 + b) for row in range(8) for a, b in choose(row // 2)]


def line_of_four(amplitudes, integrals, tile_mask):
    row = lax.axis_index("row")
    at = lax.axis_index("col")
    core, chip = row % 2, row // 2

    def after(value, *others):
        return lax.optimization_barrier((value, *others))[0]

    def across(block, bit):
        return lax.ppermute(block, "row", [(i, i ^ bit) for i in range(8)])

    def along(block, choose):
        return lax.ppermute(block, ("row", "col"), line_pairs(choose))

    inward = [(0, 1), (3, 2)]

    def first_pairs(p):
        return inward + [(1, 0)] * (p != 3) + [(2, 3)] * (p != 0)

    def second_pairs(p):
        return inward + [(1, 0)] * (p == 3) + [(2, 3)] * (p == 0)

    def relay_one(p):
        return [(1, 2 if p == 0 else 3), (2, 1 if p == 3 else 0)]

    def relay_two(p):
        return [(1, 3 if p == 0 else 2), (2, 0 if p == 3 else 1)]

    by_x, by_y, twin = across(integrals, 2), across(integrals, 4), across(integrals, 1)
    plans = jnp.asarray([plan_of(p, z) for p in range(4) for z in range(4)], jnp.int32)
    planned = lax.dynamic_slice_in_dim(plans, chip * 4 + at, 1)[0]
    facts = jnp.concatenate([planned, jnp.stack([core, chip]).astype(jnp.int32)])
    masked = apply_mask(amplitudes, tile_mask)
    by_x, by_y = after(by_x, masked, facts), after(by_y, masked, facts)
    by_both = across(after(integrals, by_x, by_y), 6)
    straight = (integrals, by_x, by_y, twin, across(by_x, 1), across(by_y, 1))
    coded, plain = ("coded",), ("plain",)
    (out_one,) = multiply(facts, masked, straight, (FIRST,), (coded,))
    one = along(out_one, first_pairs)
    (share_one,) = multiply(after(facts, out_one), masked, straight, (RELAY_ONE,), (plain,))
    columns = (*straight[:3], by_both, *straight[3:], across(after(by_both, share_one), 1))
    out_two, share_two = multiply(
        after(facts, share_one, one), masked, columns, (SECOND, RELAY_TWO), (coded, plain)
    )
    two = along(out_two, second_pairs)
    out_relay_one = add(after(facts, out_two), [(share_one, ALWAYS), (one, ALWAYS)])
    relayed_one = along(out_relay_one, relay_one)
    out_three, own = multiply(
        after(facts, out_relay_one), masked, columns, (THIRD, HERE), (coded, plain)
    )
    out_relay_two = add(after(facts, own), [(share_two, ALWAYS), (two, ALWAYS)])
    relayed_two = along(out_relay_two, relay_two)
    three = along(after(out_three, out_relay_two), lambda p: inward)
    most = add(
        after(facts, out_relay_two),
        [(own, ALWAYS), (one, OUTER), (two, OUTER), (relayed_one, ALWAYS)],
        jnp.float32,
    )
    return add(facts, [(most, ALWAYS), (three, INNER), (relayed_two, ALWAYS)], jnp.bfloat16)


def solution(mesh):
    body = line_of_four if mesh.shape["col"] == 4 and mesh.shape["row"] == 8 else general
    placed = (P("row", "col"), P("col", "row"), P("row", "col"))
    return jax.shard_map(
        body, mesh=mesh, in_specs=placed, out_specs=P("row", "col"), check_vma=False
    )
```

time: 67.3 us -> 76.1 us (1.13)
  the two profiles are of different devices: /device:TPU:10 before, /device:TPU:6 now
where the time goes in v2:
time: 76.1 us; the launch traced here: 75.8 us
  waiting for transfers between devices  39 us (51%)
  Pallas kernels  16.7 us (22%)
  starting transfers between devices  16.2 us (21%)
  local copies, waits for them, and re-layouts  2.12 us (3%)
  other arithmetic  1.67 us (2%)
    ppermute x5, waiting for transfers between devices, along(): return lax.ppermute(block, ('row', 'col'), line_pairs(choose))  23.6 us
    ppermute x7, waiting for transfers between devices, across(): return lax.ppermute(block, 'row', [(i, i ^ bit) for i in range(8)])  15.5 us
    ppermute x5, starting transfers between devices, along(): return lax.ppermute(block, ('row', 'col'), line_pairs(choose))  13.6 us
    pallas_call x4, Pallas kernels, multiply(): pl.pallas_call(functools.partial(multiply_kernel, slots, kinds, rows, wid...  12.1 us
    pallas_call x4, Pallas kernels, add(): pl.pallas_call(functools.partial(add_kernel, tuple((weight for _, weight...  4.68 us
    ppermute x7, starting transfers between devices, across(): return lax.ppermute(block, 'row', [(i, i ^ bit) for i in range(8)])  2.61 us
  transfers between devices with their start and end apart: 12, of which 8 were waited for; matrix products, arithmetic and copies ran while one was open for 4% of the time, Pallas kernels for 15%

profile of v2, /device:TPU:6, one launch (start us, length us, event | category | flops | bytes accessed | tf_op | source)
XLA Modules:
  0.0 75.8 jit_solution(11881177477543039929)
XLA Ops:
  0.0 0.0 collective-permute-start.2
  0.0 0.5 collective-permute-start.1
  0.5 0.1 collective-permute-start
  0.6 0.7 convert_element_type.3
  1.3 0.0 copy-start.1
  1.3 0.8 %dynamic-slice_bitcast_fusion = s32[9]{0:T(128)S(1)} fusion(s32[16,9]{1,0:T(8,128)} %constant.40.clone, s32[]{:T(128)S(6)} %select_n.15), kind=kLoop, calls=%fused_computation.2 | loop fusion | bytes 76 | tf_op jit(solution)/shard_map/squeeze | solution.py:230
  2.1 0.1 pad_add_fusion.facts
  2.2 0.6 mul.15
  2.8 0.7 copy-done.1
  3.5 0.0 copy-start
  3.5 0.9 %bitcast_multiply_fusion.a_ref = bf16[1024,2048]{1,0:T(8,128)(2,1)S(1)} fusion(bf16[1024,2048]{1,0:T(8,128)(2,1)S(1)} %copy-done.1, bf16[128,8,16,128]{3,2,1,0:T(8,128)(2,1)S(1)} %bitcast.8), kind=kLoop, calls=%fused_computation | loop fusion | flops 2097152 | bytes 12582912 | tf_op jit(solution)/shard_map/mul | solution.py:24
  4.4 10.1 %collective-permute-done.1.refs_2_ = bf16[2048,128]{1,0:T(8,128)(2,1)S(1)} collective-permute-done((bf16[2048,128]{1,0:T(8,128)(2,1)}, bf16[2048,128]{1,0:T(8,128)(2,1)S(1)}, u32[]{:S(2)}, u32[]{:S(2)}) %collective-permute-start.1) | collective-permute-done | bytes 524320 | tf_op jit(solution)/shard_map/ppermute | solution.py:209
  14.6 0.2 collective-permute-done.refs_1_
  14.8 0.0 collective-permute-start.3
  14.8 0.5 collective-permute-start.4
  15.3 0.0 copy-done
  15.3 1.5 %collective-permute-start.6 = (bf16[2048,128]{1,0:T(8,128)(2,1)S(1)}, bf16[2048,128]{1,0:T(8,128)(2,1)S(1)}, u32[]{:S(2)}, u32[]{:S(2)}) collective-permute-start(bf16[2048,128]{1,0:T(8,128)(2,1)S(1)} %copy-done), channel_id=1, source_target_pairs={{0,24},{4,28},{8,16},{12,20},{16,8},{20,12},{24,0},{28,4},{1,25},{... | collective-permute-start | bytes 1572872 | tf_op jit(solution)/shard_map/ppermute | solution.py:209
  16.8 0.0 collective-permute-done.2.refs_3_.refs_4_
  16.8 0.0 collective-permute-done.3.refs_4_.refs_5_
  16.8 0.6 collective-permute-done.4.refs_5_.refs_6_
  17.4 2.4 %shard_map.46 = s16[1040,256]{1,0:T(8,128)(2,1)S(1)} custom-call(s32[11]{0:T(128)S(1)} %pad_add_fusion.facts, bf16[1024,2048]{1,0:T(8,128)(2,1)S(1)} %bitcast_multiply_fusion.a_ref, bf16[2048,128]{1,0:T(8,128)(2,1)S(1)} %copy-done, bf16[2048,128]{1,0:T(8,128)(2,1)S(1)} %collective-permute-done.refs_1_, bf16[2048,128]{1,0:T(8,128)(2,1)S(1)} %collective-permute-done.1.refs_2_, ...), custom_call_target="tpu_custom_call" | custom-call | flops 3000000000 | bytes 9000000 | tf_op jit(solution)/shard_map/pallas_call | solution.py:118
  19.8 3.5 %collective-permute-start.5 = (s16[1040,256]{1,0:T(8,128)(2,1)S(1)}, s16[1040,256]{1,0:T(8,128)(2,1)S(1)}, u32[]{:S(2)}, u32[]{:S(2)}) collective-permute-start(s16[1040,256]{1,0:T(8,128)(2,1)S(1)} %shard_map.46), channel_id=1, source_target_pairs={{0,1},{3,2},{1,0},{4,5},{7,6},{5,4},{8,9},{11,10},{9,8},{10,11},{1... | collective-permute-start | bytes 1597448 | tf_op jit(solution)/shard_map/ppermute | solution.py:212
  23.3 2.2 %shard_map.47.refs_0_ = f32[1024,256]{1,0:T(8,128)S(1)} custom-call(s32[11]{0:T(128)S(1)} %pad_add_fusion.facts, bf16[1024,2048]{1,0:T(8,128)(2,1)S(1)} %bitcast_multiply_fusion.a_ref, bf16[2048,128]{1,0:T(8,128)(2,1)S(1)} %copy-done, bf16[2048,128]{1,0:T(8,128)(2,1)S(1)} %collective-permute-done.refs_1_, ...), custom_call_target="tpu_custom_call" | custom-call | flops 3000000000 | bytes 9000000 | tf_op jit(solution)/shard_map/pallas_call | solution.py:118
  25.6 4.4 %collective-permute-done.6.refs_3_ = bf16[2048,128]{1,0:T(8,128)(2,1)S(1)} collective-permute-done((bf16[2048,128]{1,0:T(8,128)(2,1)S(1)}, bf16[2048,128]{1,0:T(8,128)(2,1)S(1)}, u32[]{:S(2)}, u32[]{:S(2)}) %collective-permute-start.6) | collective-permute-done | bytes 524320 | tf_op jit(solution)/shard_map/ppermute | solution.py:209
  30.0 0.0 collective-permute-start.7
  30.0 4.9 %collective-permute-done.5.refs_1_ = s16[1040,256]{1,0:T(8,128)(2,1)S(1)} collective-permute-done((s16[1040,256]{1,0:T(8,128)(2,1)S(1)}, s16[1040,256]{1,0:T(8,128)(2,1)S(1)}, u32[]{:S(2)}, u32[]{:S(2)}) %collective-permute-start.5) | collective-permute-done | bytes 532512 | tf_op jit(solution)/shard_map/ppermute | solution.py:212
  34.9 0.0 collective-permute-done.7.refs_7_
  34.9 3.7 %shard_map.48 = (s16[1040,256]{1,0:T(8,128)(2,1)S(1)}, f32[1024,256]{1,0:T(8,128)S(1)}) custom-call(s32[11]{0:T(128)S(1)} %pad_add_fusion.facts, bf16[1024,2048]{1,0:T(8,128)(2,1)S(1)} %bitcast_multiply_fusion.a_ref, bf16[2048,128]{1,0:T(8,128)(2,1)S(1)} %copy-done, bf16[2048,128]{1,0:T(8,128)(2,1)S(1)} %collective-permute-done.refs_1_, ...), custom_call_target="tpu_custom_call" | custom-call | flops 3000000000 | bytes 9000000 | tf_op jit(solution)/shard_map/pallas_call | solution.py:118
  38.7 4.4 %collective-permute-start.8 = (s16[1040,256]{1,0:T(8,128)(2,1)S(1)}, s16[1040,256]{1,0:T(8,128)(2,1)S(1)}, u32[]{:S(2)}, u32[]{:S(2)}) collective-permute-start(s16[1040,256]{1,0:T(8,128)(2,1)S(1)} %get-tuple-element.26), channel_id=1, source_target_pairs={{0,1},{3,2},{2,3},{4,5},{7,6},{6,7},{8,9},{11,10},{12,13},{15,14},... | collective-permute-start | bytes 1597448 | tf_op jit(solution)/shard_map/ppermute | solution.py:212
  43.1 1.0 %shard_map.49 = s16[1040,256]{1,0:T(8,128)(2,1)S(1)} custom-call(s32[11]{0:T(128)S(1)} %pad_add_fusion.facts, f32[1024,256]{1,0:T(8,128)S(1)} %shard_map.47.refs_0_, s16[1040,256]{1,0:T(8,128)(2,1)S(1)} %collective-permute-done.5.refs_1_), custom_call_target="tpu_custom_call" | custom-call | flops 3000000000 | bytes 9000000 | tf_op jit(solution)/shard_map/pallas_call | solution.py:163
  44.1 0.7 collective-permute-start.9
  44.8 3.7 %shard_map.50 = (s16[1040,256]{1,0:T(8,128)(2,1)S(1)}, f32[1024,256]{1,0:T(8,128)S(1)}) custom-call(s32[11]{0:T(128)S(1)} %pad_add_fusion.facts, bf16[1024,2048]{1,0:T(8,128)(2,1)S(1)} %bitcast_multiply_fusion.a_ref, bf16[2048,128]{1,0:T(8,128)(2,1)S(1)} %copy-done, bf16[2048,128]{1,0:T(8,128)(2,1)S(1)} %collective-permute-done.refs_1_, ...), custom_call_target="tpu_custom_call" | custom-call | flops 3000000000 | bytes 9000000 | tf_op jit(solution)/shard_map/pallas_call | solution.py:118
  48.5 6.1 %collective-permute-done.8.refs_1_.refs_2_ = s16[1040,256]{1,0:T(8,128)(2,1)S(1)} collective-permute-done((s16[1040,256]{1,0:T(8,128)(2,1)S(1)}, s16[1040,256]{1,0:T(8,128)(2,1)S(1)}, u32[]{:S(2)}, u32[]{:S(2)}) %collective-permute-start.8) | collective-permute-done | bytes 532512 | tf_op jit(solution)/shard_map/ppermute | solution.py:212
  54.6 1.0 %shard_map.51 = s16[1040,256]{1,0:T(8,128)(2,1)S(1)} custom-call(s32[11]{0:T(128)S(1)} %pad_add_fusion.facts, f32[1024,256]{1,0:T(8,128)S(1)} %get-tuple-element.31.refs_0_, s16[1040,256]{1,0:T(8,128)(2,1)S(1)} %collective-permute-done.8.refs_1_.refs_2_), custom_call_target="tpu_custom_call" | custom-call | flops 3000000000 | bytes 9000000 | tf_op jit(solution)/shard_map/pallas_call | solution.py:163
  55.6 3.7 %collective-permute-start.10 = (s16[1040,256]{1,0:T(8,128)(2,1)S(1)}, s16[1040,256]{1,0:T(8,128)(2,1)S(1)}, u32[]{:S(2)}, u32[]{:S(2)}) collective-permute-start(s16[1040,256]{1,0:T(8,128)(2,1)S(1)} %get-tuple-element.34), channel_id=1, source_target_pairs={{0,1},{3,2},{4,5},{7,6},{8,9},{11,10},{12,13},{15,14},{16,17},{19,... | collective-permute-start | bytes 1597448 | tf_op jit(solution)/shard_map/ppermute | solution.py:212
  59.3 1.3 %collective-permute-start.11 = (s16[1040,256]{1,0:T(8,128)(2,1)S(1)}, s16[1040,256]{1,0:T(8,128)(2,1)S(1)}, u32[]{:S(2)}, u32[]{:S(2)}) collective-permute-start(s16[1040,256]{1,0:T(8,128)(2,1)S(1)} %shard_map.51), channel_id=1, source_target_pairs={{1,3},{2,1},{5,7},{6,5},{9,10},{10,9},{13,14},{14,13},{17,18},{18,... | collective-permute-start | bytes 1597448 | tf_op jit(solution)/shard_map/ppermute | solution.py:212
  60.6 0.0 collective-permute-done.9.refs_3_
  60.6 1.1 %shard_map.52.refs_0_ = f32[1024,256]{1,0:T(8,128)S(1)} custom-call(s32[11]{0:T(128)S(1)} %pad_add_fusion.facts, f32[1024,256]{1,0:T(8,128)S(1)} %get-tuple-element.29.refs_0_, s16[1040,256]{1,0:T(8,128)(2,1)S(1)} %collective-permute-done.5.refs_1_, s16[1040,256]{1,0:T(8,128)(2,1)S(1)} %collective-permute-done.8.refs_1_.refs_2_, ...), custom_call_target="tpu_custom_call" | custom-call | flops 3000000000 | bytes 9000000 | tf_op jit(solution)/shard_map/pallas_call | solution.py:163
  61.7 7.5 %collective-permute-done.10.refs_1_ = s16[1040,256]{1,0:T(8,128)(2,1)S(1)} collective-permute-done((s16[1040,256]{1,0:T(8,128)(2,1)S(1)}, s16[1040,256]{1,0:T(8,128)(2,1)S(1)}, u32[]{:S(2)}, u32[]{:S(2)}) %collective-permute-start.10) | collective-permute-done | bytes 532512 | tf_op jit(solution)/shard_map/ppermute | solution.py:212
  69.2 5.0 %collective-permute-done.11.refs_2_ = s16[1040,256]{1,0:T(8,128)(2,1)S(1)} collective-permute-done((s16[1040,256]{1,0:T(8,128)(2,1)S(1)}, s16[1040,256]{1,0:T(8,128)(2,1)S(1)}, u32[]{:S(2)}, u32[]{:S(2)}) %collective-permute-start.11) | collective-permute-done | bytes 532512 | tf_op jit(solution)/shard_map/ppermute | solution.py:212
  74.2 1.6 %shard_map.53 = bf16[1024,256]{1,0:T(8,128)(2,1)} custom-call(s32[11]{0:T(128)S(1)} %pad_add_fusion.facts, f32[1024,256]{1,0:T(8,128)S(1)} %shard_map.52.refs_0_, s16[1040,256]{1,0:T(8,128)(2,1)S(1)} %collective-permute-done.10.refs_1_, s16[1040,256]{1,0:T(8,128)(2,1)S(1)} %collective-permute-done.11.refs_2_), custom_call_target="tpu_custom_call" | custom-call | flops 3000000000 | bytes 9000000 | tf_op jit(solution)/shard_map/pallas_call | solution.py:163
Async XLA Ops:
  0.0 16.8 %collective-permute-start.2 = (bf16[2048,128]{1,0:T(8,128)(2,1)}, bf16[2048,128]{1,0:T(8,128)(2,1)S(1)}, u32[]{:S(2)}, u32[]{:S(2)}) collective-permute-start(bf16[2048,128]{1,0:T(8,128)(2,1)} %refs_0_.7), channel_id=1, source_target_pairs={{0,4},{4,0},{8,12},{12,8},{16,20},{20,16},{24,28},{28,24},{1,5},{5... | collective-permute-start | bytes 1572872 | tf_op jit(solution)/shard_map/ppermute | solution.py:209
  0.0 14.5 %collective-permute-start.1 = (bf16[2048,128]{1,0:T(8,128)(2,1)}, bf16[2048,128]{1,0:T(8,128)(2,1)S(1)}, u32[]{:S(2)}, u32[]{:S(2)}) collective-permute-start(bf16[2048,128]{1,0:T(8,128)(2,1)} %refs_0_.7), channel_id=1, source_target_pairs={{0,16},{4,20},{8,24},{12,28},{16,0},{20,4},{24,8},{28,12},{1,17},{... | collective-permute-start | bytes 1572872 | tf_op jit(solution)/shard_map/ppermute | solution.py:209
  0.5 14.3 %collective-permute-start = (bf16[2048,128]{1,0:T(8,128)(2,1)}, bf16[2048,128]{1,0:T(8,128)(2,1)S(1)}, u32[]{:S(2)}, u32[]{:S(2)}) collective-permute-start(bf16[2048,128]{1,0:T(8,128)(2,1)} %refs_0_.7), channel_id=1, source_target_pairs={{0,8},{4,12},{8,0},{12,4},{16,24},{20,28},{24,16},{28,20},{1,9},{5... | collective-permute-start | bytes 1572872 | tf_op jit(solution)/shard_map/ppermute | solution.py:209
  1.3 2.2 %copy-start.1 = (bf16[1024,2048]{1,0:T(8,128)(2,1)S(1)}, bf16[1024,2048]{1,0:T(8,128)(2,1)}, u32[]{:S(2)}) copy-start(bf16[1024,2048]{1,0:T(8,128)(2,1)} %param.4) | copy-start | bytes 12582916
  3.5 11.8 %copy-start = (bf16[2048,128]{1,0:T(8,128)(2,1)S(1)}, bf16[2048,128]{1,0:T(8,128)(2,1)}, u32[]{:S(2)}) copy-start(bf16[2048,128]{1,0:T(8,128)(2,1)} %refs_0_.7) | copy-start | bytes 1572868
  14.8 2.0 %collective-permute-start.3 = (bf16[2048,128]{1,0:T(8,128)(2,1)S(1)}, bf16[2048,128]{1,0:T(8,128)(2,1)S(1)}, u32[]{:S(2)}, u32[]{:S(2)}) collective-permute-start(bf16[2048,128]{1,0:T(8,128)(2,1)S(1)} %collective-permute-done.refs_1_), channel_id=1, source_target_pairs={{0,4},{4,0},{8,12},{12,8},{16,20},{20,16},{24,28},{28,24},{1,5},{5... | collective-permute-start | bytes 1572872 | tf_op jit(solution)/shard_map/ppermute | solution.py:209
  14.8 2.7 %collective-permute-start.4 = (bf16[2048,128]{1,0:T(8,128)(2,1)S(1)}, bf16[2048,128]{1,0:T(8,128)(2,1)S(1)}, u32[]{:S(2)}, u32[]{:S(2)}) collective-permute-start(bf16[2048,128]{1,0:T(8,128)(2,1)S(1)} %collective-permute-done.1.refs_2_), channel_id=1, source_target_pairs={{0,4},{4,0},{8,12},{12,8},{16,20},{20,16},{24,28},{28,24},{1,5},{5... | collective-permute-start | bytes 1572872 | tf_op jit(solution)/shard_map/ppermute | solution.py:209
  15.3 14.7 %collective-permute-start.6 = (bf16[2048,128]{1,0:T(8,128)(2,1)S(1)}, bf16[2048,128]{1,0:T(8,128)(2,1)S(1)}, u32[]{:S(2)}, u32[]{:S(2)}) collective-permute-start(bf16[2048,128]{1,0:T(8,128)(2,1)S(1)} %copy-done), channel_id=1, source_target_pairs={{0,24},{4,28},{8,16},{12,20},{16,8},{20,12},{24,0},{28,4},{1,25},{... | collective-permute-start | bytes 1572872 | tf_op jit(solution)/shard_map/ppermute | solution.py:209
  19.8 15.1 %collective-permute-start.5 = (s16[1040,256]{1,0:T(8,128)(2,1)S(1)}, s16[1040,256]{1,0:T(8,128)(2,1)S(1)}, u32[]{:S(2)}, u32[]{:S(2)}) collective-permute-start(s16[1040,256]{1,0:T(8,128)(2,1)S(1)} %shard_map.46), channel_id=1, source_target_pairs={{0,1},{3,2},{1,0},{4,5},{7,6},{5,4},{8,9},{11,10},{9,8},{10,11},{1... | collective-permute-start | bytes 1597448 | tf_op jit(solution)/shard_map/ppermute | solution.py:212
  30.0 4.9 %collective-permute-start.7 = (bf16[2048,128]{1,0:T(8,128)(2,1)S(1)}, bf16[2048,128]{1,0:T(8,128)(2,1)S(1)}, u32[]{:S(2)}, u32[]{:S(2)}) collective-permute-start(bf16[2048,128]{1,0:T(8,128)(2,1)S(1)} %collective-permute-done.6.refs_3_), channel_id=1, source_target_pairs={{0,4},{4,0},{8,12},{12,8},{16,20},{20,16},{24,28},{28,24},{1,5},{5... | collective-permute-start | bytes 1572872 | tf_op jit(solution)/shard_map/ppermute | solution.py:209
  38.7 16.0 %collective-permute-start.8 = (s16[1040,256]{1,0:T(8,128)(2,1)S(1)}, s16[1040,256]{1,0:T(8,128)(2,1)S(1)}, u32[]{:S(2)}, u32[]{:S(2)}) collective-permute-start(s16[1040,256]{1,0:T(8,128)(2,1)S(1)} %get-tuple-element.26), channel_id=1, source_target_pairs={{0,1},{3,2},{2,3},{4,5},{7,6},{6,7},{8,9},{11,10},{12,13},{15,14},... | collective-permute-start | bytes 1597448 | tf_op jit(solution)/shard_map/ppermute | solution.py:212
  44.1 16.5 %collective-permute-start.9 = (s16[1040,256]{1,0:T(8,128)(2,1)S(1)}, s16[1040,256]{1,0:T(8,128)(2,1)S(1)}, u32[]{:S(2)}, u32[]{:S(2)}) collective-permute-start(s16[1040,256]{1,0:T(8,128)(2,1)S(1)} %shard_map.49), channel_id=1, source_target_pairs={{1,2},{2,0},{5,6},{6,4},{9,11},{10,8},{13,15},{14,12},{17,19},{18,... | collective-permute-start | bytes 1597448 | tf_op jit(solution)/shard_map/ppermute | solution.py:212
  55.6 13.5 %collective-permute-start.10 = (s16[1040,256]{1,0:T(8,128)(2,1)S(1)}, s16[1040,256]{1,0:T(8,128)(2,1)S(1)}, u32[]{:S(2)}, u32[]{:S(2)}) collective-permute-start(s16[1040,256]{1,0:T(8,128)(2,1)S(1)} %get-tuple-element.34), channel_id=1, source_target_pairs={{0,1},{3,2},{4,5},{7,6},{8,9},{11,10},{12,13},{15,14},{16,17},{19,... | collective-permute-start | bytes 1597448 | tf_op jit(solution)/shard_map/ppermute | solution.py:212
  59.3 14.9 %collective-permute-start.11 = (s16[1040,256]{1,0:T(8,128)(2,1)S(1)}, s16[1040,256]{1,0:T(8,128)(2,1)S(1)}, u32[]{:S(2)}, u32[]{:S(2)}) collective-permute-start(s16[1040,256]{1,0:T(8,128)(2,1)S(1)} %shard_map.51), channel_id=1, source_target_pairs={{1,3},{2,1},{5,7},{6,5},{9,10},{10,9},{13,14},{14,13},{17,18},{18,... | collective-permute-start | bytes 1597448 | tf_op jit(solution)/shard_map/ppermute | solution.py:212
